TPU v7x, 32 devices: a whole 2x2x4 slice. The times are simulated.
32 devices in a mesh: vec: 4 (over y, core), row: 2 (over x), col: 4 (over z).
Axes of the slice: x: 2, y: 2, z: 4, core: 2. Of those that a mesh axis runs over, the one named last changes fastest.
Arguments:
- checkpoints: float32 [2, 2, 16, 64, 512], P(None, None, 'vec', 'row', 'col'), may hold values from -6 to 6
- adjoints_in: float32 [2, 16, 64, 512], P(None, 'vec', 'row', 'col'), may hold values from -4 to 4
- vector_bits: int32 [16, 64, 512], P('vec', 'row', 'col'), may hold values 0 or 1
- potential_int: int32 [64, 512], P('row', 'col'), may hold values from -32767 to 32767
- pot_scale: float32 [1], replicated, may hold values from 1.5e-05 to 9e-05
- energies: float32 [16], replicated, may hold values from -0.9 to 0.9
- residual: float32 [16, 64, 512], P(None, 'row', 'col'), may hold values from -6 to 6
- first_segment: int32 [1], replicated, may hold values from 0 to 62
Outputs:
- potential_grad: float32 [64, 512], P('row', 'col')
- adjoint_out: float32 [2, 16, 64, 512], P(None, 'vec', 'row', 'col')
All inputs are finite; a program needn't handle non-finite values. No bound on the sum of `vector_bits` on one device may be relied on, other than what follows from the above.
Results may differ from a plain program's by a relative error of at most 0.0003.
Values sent between devices are 32-bit elements; how exact they have to be, the bound alone decides.
A program may use at most 64 MiB of HBM per device.

v0:
```python
import math

import jax
import jax.numpy as jnp
from jax import lax
from jax.sharding import PartitionSpec as P

SEG = 16
MOMENTS = 1024
QMAX = 32767


def extended_2(value, sides, width):
    for axis, dim in sides:
        devices, length = (lax.axis_size(axis), value.shape[dim])
        up = [(i, (i + 1) % devices) for i in range(devices)]
        down = [(j, i) for i, j in up]
        last = lax.slice_in_dim(value, length - width, length, axis=dim)
        initial = lax.slice_in_dim(value, 0, width, axis=dim)
        before = lax.ppermute(last, axis, up)
        after = lax.ppermute(initial, axis, down)
        value = jnp.concatenate([before, value, after], axis=dim)
    return value


def window_coefs(first_segment, energies):
    moment_order = first_segment[0] * SEG + jnp.arange(2 * SEG, dtype=jnp.int32)
    degree = moment_order.astype(jnp.float32)
    kernel_norm = float(MOMENTS + 1)
    angle_step = math.pi / kernel_norm
    jackson = (
        (kernel_norm - degree) * jnp.cos(angle_step * degree)
        + jnp.sin(angle_step * degree) * (math.cos(angle_step) / math.sin(angle_step))
    ) / kernel_norm
    factor = jnp.where(moment_order == 0, 1.0, 2.0).astype(jnp.float32)
    angles = jnp.arccos(energies)
    cosines = jnp.cos(degree[:, None] * angles[None, :])
    return (jackson * factor)[:, None] * cosines / (math.pi * jnp.sin(angles))[None, :]


def stencil(extended, onsite, inv_span):
    middle = extended[..., 1:-1, 1:-1]
    beside = (
        extended[..., 2:, 1:-1]
        + extended[..., :-2, 1:-1]
        + extended[..., 1:-1, 2:]
        + extended[..., 1:-1, :-2]
    )
    return inv_span * (onsite * middle - beside)


def per_device(
    checkpoints,
    adjoints_in,
    vector_bits,
    potential_int,
    pot_scale,
    energies,
    residual,
    first_segment,
):
    pot_factor = pot_scale[0]
    inv_span = 1.0 / (4.5 + QMAX * pot_factor)
    onsite = potential_int.astype(jnp.float32) * pot_factor
    coefficients = window_coefs(first_segment, energies)
    vector_count = lax.axis_size("vec") * vector_bits.shape[0]
    inv_count = 1.0 / vector_count
    sign_weights = (2 * vector_bits - 1).astype(jnp.float32) * inv_count
    earlier = checkpoints[:, 0]
    current = checkpoints[:, 1]
    zero_grad = jnp.zeros(onsite.shape, jnp.float32)
    carried = (adjoints_in[0], adjoints_in[1], zero_grad)
    weights = jnp.einsum("ne,eij->nij", coefficients, residual, precision=lax.Precision.HIGHEST)

    def forward_step(pair_state, unused):
        before, now = pair_state
        padded = extended_2(now, (("row", 2), ("col", 3)), 1)
        advanced = 2.0 * stencil(padded, onsite, inv_span) - before
        return ((now, advanced), advanced)

    _, generated = lax.scan(forward_step, (earlier, current), None, length=SEG - 2)
    states = jnp.concatenate([earlier[None], current[None], generated], axis=0)

    def adjoint_step(step_carry, inputs):
        after_one, after_two, accum_grad = step_carry
        state_now, weight_now = inputs
        padded = extended_2(after_one, (("row", 1), ("col", 2)), 1)
        accum_grad = accum_grad + jnp.sum(after_one * state_now, axis=0)
        advanced = weight_now * sign_weights + 2.0 * stencil(padded, onsite, inv_span) - after_two
        return ((advanced, after_one, accum_grad), None)

    for segment in (1, 0):
        carried, _ = lax.scan(
            adjoint_step,
            carried,
            (states[:, segment], weights[segment * SEG : (segment + 1) * SEG]),
            reverse=True,
        )
    adjoint_zero, adjoint_first, accum_grad = carried
    gradient = lax.psum(accum_grad, "vec") * (2.0 * inv_span)
    return (gradient, jnp.stack([adjoint_zero, adjoint_first]))


def solution(mesh):
    return jax.shard_map(
        per_device,
        mesh=mesh,
        in_specs=(
            P(None, None, "vec", "row", "col"),
            P(None, "vec", "row", "col"),
            P("vec", "row", "col"),
            P("row", "col"),
            P(),
            P(),
            P(None, "row", "col"),
            P(),
        ),
        out_specs=(P("row", "col"), P(None, "vec", "row", "col")),
        check_vma=False,
    )
```

profile of v0, /device:TPU:0, one launch (start us, length us, event | category | flops | bytes accessed | tf_op | source)
XLA Modules:
  0.0 592.7 jit_solution(9715257806480630211)
XLA Ops:
  3.1 198.6 %while.51 = (s32[]{:T(128)}, f32[2,4,32,128]{3,2,1,0:T(8,128)S(1)}, f32[2,4,32,128]{3,2,1,0:T(8,128)S(1)}, f32[14,2,4,32,128]{4,3,2,0,1:T(8,128)S(1)}, f32[]{:T(128)}, /*index=5*/f32[32,128]{1,0:T(8,128)S(1)}, s32[]{:T(128)}) while((s32[]{:T(128)}, f32[2,4,32,128]{3,2,1,0:T(8,128)S(1)}, f32[2,4,32,128]{3,2,1,0:T(8,128)S(1)}, ...), condition=%wide.region_1.2_spmd, body=%wide.region_0.1_spmd.sunk | while | flops 593922 | bytes 1741821 | solution.py:81
  3.1 3.0 collective-permute-start
  13.8 4.7 collective-permute-done.2
  27.8 3.8 collective-permute-done.2
  38.5 3.3 collective-permute-start.3
  41.8 3.5 collective-permute-done.2
  53.9 3.5 collective-permute-done.2
  57.3 4.4 collective-permute-done.3
  68.7 2.8 collective-permute-start.3
  71.6 4.8 collective-permute-done.2
  81.9 3.1 collective-permute-start.3
  85.1 3.5 collective-permute-done.2
  98.3 3.5 collective-permute-done.2
  108.6 3.3 collective-permute-start.3
  112.0 4.2 collective-permute-done.2
  117.8 3.2 collective-permute-start
  125.3 3.3 collective-permute-start.3
  128.6 4.7 collective-permute-done.2
  142.1 3.5 collective-permute-done.2
  153.5 3.1 collective-permute-start.3
  156.6 3.5 collective-permute-done.2
  166.0 2.8 collective-permute-start.3
  168.8 3.4 collective-permute-done.2
  182.7 4.7 collective-permute-done.2
  196.5 3.5 collective-permute-done.2
  203.9 190.0 %while.53 = (s32[]{:T(128)}, f32[4,32,128]{2,1,0:T(8,128)S(1)}, f32[4,32,128]{2,1,0:T(8,128)S(1)}, f32[32,128]{1,0:T(8,128)S(1)}, f32[16,32,128]{2,0,1:T(8,128)S...) while((s32[]{:T(128)}, f32[4,32,128]{2,1,0:T(8,128)S(1)}, ...), condition=%wide.region_4.5_spmd.clone, body=%wide.region_2.4_spmd.clone.sunk | while | flops 366596 | bytes 962295 | solution.py:93
  209.8 3.3 collective-permute-start.11
  244.9 3.1 collective-permute-start.11
  248.0 3.1 collective-permute-done.10
  269.1 3.3 collective-permute-start.11
  295.6 3.3 collective-permute-done.10
  304.6 2.9 collective-permute-start.11
  316.2 2.9 collective-permute-start.11
  327.8 3.0 collective-permute-start.11
  330.8 3.3 collective-permute-done.10
  352.2 3.2 collective-permute-start.11
  375.7 3.3 collective-permute-start.11
  379.0 3.2 collective-permute-done.10
  388.2 3.0 collective-permute-start.11
  394.0 187.3 %while.52 = (s32[]{:T(128)}, f32[4,32,128]{2,1,0:T(8,128)S(1)}, f32[4,32,128]{2,1,0:T(8,128)S(1)}, f32[32,128]{1,0:T(8,128)S(1)}, f32[16,32,128]{2,0,1:T(8,128)S...) while((s32[]{:T(128)}, f32[4,32,128]{2,1,0:T(8,128)S(1)}, ...), condition=%wide.region_7.8_spmd, body=%wide.region_5.7_spmd.sunk | while | flops 362499 | bytes 962277 | solution.py:93
  400.0 3.0 collective-permute-start.7
  462.6 3.0 collective-permute-done.6
  483.2 3.2 collective-permute-start.7
  506.7 2.8 collective-permute-start.7
  529.7 2.8 collective-permute-start.7
  552.8 2.8 collective-permute-start.7
  575.8 2.8 collective-permute-start.7
  582.0 10.1 %psum.7 = f32[32,128]{1,0:T(8,128)S(1)} all-reduce(f32[32,128]{1,0:T(8,128)S(1)} %get-tuple-element.400), channel_id=1, replica_groups=mesh['vec'=4,'row'=2,'col'=4] {'vec'}, use_global_device_ids=true, to_apply=%region_8.9 | all-reduce | flops 4096 | bytes 32768 | tf_op jit(solution)/shard_map/psum | solution.py:100
  (719 shorter events, 429.1 us)
Async XLA Ops:
  9.9 8.6 %collective-permute-start.2 = (f32[2,4,34,1]{3,2,1,0:T(8,128)S(1)}, f32[2,4,34,1]{3,2,1,0:T(8,128)S(1)}, u32[]{:S(2)}, u32[]{:S(2)}) collective-permute-start(f32[2,4,34,1]{3,2,1,0:T(8,128)S(1)} %get-tuple-element.670), channel_id=1, source_target_pairs={{0,1},{1,2},{2,3},{3,0},{4,5},{5,6},{6,7},{7,4},{8,9},{9,10},{10,1... | collective-permute-start | bytes 3272 | tf_op jit(solution)/shard_map/while/body/eval_jaxpr/ppermute | solution.py:20
  11.5 8.0 %collective-permute-start.3 = (f32[2,4,34,1]{3,2,1,0:T(8,128)S(1)}, f32[2,4,34,1]{3,2,1,0:T(8,128)S(1)}, u32[]{:S(2)}, u32[]{:S(2)}) collective-permute-start(f32[2,4,34,1]{3,2,1,0:T(8,128)S(1)} %get-tuple-element.671), channel_id=1, source_target_pairs={{1,0},{2,1},{3,2},{0,3},{5,4},{6,5},{7,6},{4,7},{9,8},{10,9},{11,1... | collective-permute-start | bytes 3272 | tf_op jit(solution)/shard_map/while/body/eval_jaxpr/ppermute | solution.py:21
  23.9 7.7 %collective-permute-start.2 = (f32[2,4,34,1]{3,2,1,0:T(8,128)S(1)}, f32[2,4,34,1]{3,2,1,0:T(8,128)S(1)}, u32[]{:S(2)}, u32[]{:S(2)}) collective-permute-start(f32[2,4,34,1]{3,2,1,0:T(8,128)S(1)} %get-tuple-element.670), channel_id=1, source_target_pairs={{0,1},{1,2},{2,3},{3,0},{4,5},{5,6},{6,7},{7,4},{8,9},{9,10},{10,1... | collective-permute-start | bytes 3272 | tf_op jit(solution)/shard_map/while/body/eval_jaxpr/ppermute | solution.py:20
  25.1 7.1 %collective-permute-start.3 = (f32[2,4,34,1]{3,2,1,0:T(8,128)S(1)}, f32[2,4,34,1]{3,2,1,0:T(8,128)S(1)}, u32[]{:S(2)}, u32[]{:S(2)}) collective-permute-start(f32[2,4,34,1]{3,2,1,0:T(8,128)S(1)} %get-tuple-element.671), channel_id=1, source_target_pairs={{1,0},{2,1},{3,2},{0,3},{5,4},{6,5},{7,6},{4,7},{9,8},{10,9},{11,1... | collective-permute-start | bytes 3272 | tf_op jit(solution)/shard_map/while/body/eval_jaxpr/ppermute | solution.py:21
  37.9 7.3 %collective-permute-start.2 = (f32[2,4,34,1]{3,2,1,0:T(8,128)S(1)}, f32[2,4,34,1]{3,2,1,0:T(8,128)S(1)}, u32[]{:S(2)}, u32[]{:S(2)}) collective-permute-start(f32[2,4,34,1]{3,2,1,0:T(8,128)S(1)} %get-tuple-element.670), channel_id=1, source_target_pairs={{0,1},{1,2},{2,3},{3,0},{4,5},{5,6},{6,7},{7,4},{8,9},{9,10},{10,1... | collective-permute-start | bytes 3272 | tf_op jit(solution)/shard_map/while/body/eval_jaxpr/ppermute | solution.py:20
  38.5 7.1 %collective-permute-start.3 = (f32[2,4,34,1]{3,2,1,0:T(8,128)S(1)}, f32[2,4,34,1]{3,2,1,0:T(8,128)S(1)}, u32[]{:S(2)}, u32[]{:S(2)}) collective-permute-start(f32[2,4,34,1]{3,2,1,0:T(8,128)S(1)} %get-tuple-element.671), channel_id=1, source_target_pairs={{1,0},{2,1},{3,2},{0,3},{5,4},{6,5},{7,6},{4,7},{9,8},{10,9},{11,1... | collective-permute-start | bytes 3272 | tf_op jit(solution)/shard_map/while/body/eval_jaxpr/ppermute | solution.py:21
  50.0 7.3 %collective-permute-start.2 = (f32[2,4,34,1]{3,2,1,0:T(8,128)S(1)}, f32[2,4,34,1]{3,2,1,0:T(8,128)S(1)}, u32[]{:S(2)}, u32[]{:S(2)}) collective-permute-start(f32[2,4,34,1]{3,2,1,0:T(8,128)S(1)} %get-tuple-element.670), channel_id=1, source_target_pairs={{0,1},{1,2},{2,3},{3,0},{4,5},{5,6},{6,7},{7,4},{8,9},{9,10},{10,1... | collective-permute-start | bytes 3272 | tf_op jit(solution)/shard_map/while/body/eval_jaxpr/ppermute | solution.py:20
  51.7 10.0 %collective-permute-start.3 = (f32[2,4,34,1]{3,2,1,0:T(8,128)S(1)}, f32[2,4,34,1]{3,2,1,0:T(8,128)S(1)}, u32[]{:S(2)}, u32[]{:S(2)}) collective-permute-start(f32[2,4,34,1]{3,2,1,0:T(8,128)S(1)} %get-tuple-element.671), channel_id=1, source_target_pairs={{1,0},{2,1},{3,2},{0,3},{5,4},{6,5},{7,6},{4,7},{9,8},{10,9},{11,1... | collective-permute-start | bytes 3272 | tf_op jit(solution)/shard_map/while/body/eval_jaxpr/ppermute | solution.py:21
  67.7 8.6 %collective-permute-start.2 = (f32[2,4,34,1]{3,2,1,0:T(8,128)S(1)}, f32[2,4,34,1]{3,2,1,0:T(8,128)S(1)}, u32[]{:S(2)}, u32[]{:S(2)}) collective-permute-start(f32[2,4,34,1]{3,2,1,0:T(8,128)S(1)} %get-tuple-element.670), channel_id=1, source_target_pairs={{0,1},{1,2},{2,3},{3,0},{4,5},{5,6},{6,7},{7,4},{8,9},{9,10},{10,1... | collective-permute-start | bytes 3272 | tf_op jit(solution)/shard_map/while/body/eval_jaxpr/ppermute | solution.py:20
  68.7 8.0 %collective-permute-start.3 = (f32[2,4,34,1]{3,2,1,0:T(8,128)S(1)}, f32[2,4,34,1]{3,2,1,0:T(8,128)S(1)}, u32[]{:S(2)}, u32[]{:S(2)}) collective-permute-start(f32[2,4,34,1]{3,2,1,0:T(8,128)S(1)} %get-tuple-element.671), channel_id=1, source_target_pairs={{1,0},{2,1},{3,2},{0,3},{5,4},{6,5},{7,6},{4,7},{9,8},{10,9},{11,1... | collective-permute-start | bytes 3272 | tf_op jit(solution)/shard_map/while/body/eval_jaxpr/ppermute | solution.py:21
  81.2 7.3 %collective-permute-start.2 = (f32[2,4,34,1]{3,2,1,0:T(8,128)S(1)}, f32[2,4,34,1]{3,2,1,0:T(8,128)S(1)}, u32[]{:S(2)}, u32[]{:S(2)}) collective-permute-start(f32[2,4,34,1]{3,2,1,0:T(8,128)S(1)} %get-tuple-element.670), channel_id=1, source_target_pairs={{0,1},{1,2},{2,3},{3,0},{4,5},{5,6},{6,7},{7,4},{8,9},{9,10},{10,1... | collective-permute-start | bytes 3272 | tf_op jit(solution)/shard_map/while/body/eval_jaxpr/ppermute | solution.py:20
  81.9 7.1 %collective-permute-start.3 = (f32[2,4,34,1]{3,2,1,0:T(8,128)S(1)}, f32[2,4,34,1]{3,2,1,0:T(8,128)S(1)}, u32[]{:S(2)}, u32[]{:S(2)}) collective-permute-start(f32[2,4,34,1]{3,2,1,0:T(8,128)S(1)} %get-tuple-element.671), channel_id=1, source_target_pairs={{1,0},{2,1},{3,2},{0,3},{5,4},{6,5},{7,6},{4,7},{9,8},{10,9},{11,1... | collective-permute-start | bytes 3272 | tf_op jit(solution)/shard_map/while/body/eval_jaxpr/ppermute | solution.py:21
  94.4 7.3 %collective-permute-start.2 = (f32[2,4,34,1]{3,2,1,0:T(8,128)S(1)}, f32[2,4,34,1]{3,2,1,0:T(8,128)S(1)}, u32[]{:S(2)}, u32[]{:S(2)}) collective-permute-start(f32[2,4,34,1]{3,2,1,0:T(8,128)S(1)} %get-tuple-element.670), channel_id=1, source_target_pairs={{0,1},{1,2},{2,3},{3,0},{4,5},{5,6},{6,7},{7,4},{8,9},{9,10},{10,1... | collective-permute-start | bytes 3272 | tf_op jit(solution)/shard_map/while/body/eval_jaxpr/ppermute | solution.py:20
  96.4 7.5 %collective-permute-start.3 = (f32[2,4,34,1]{3,2,1,0:T(8,128)S(1)}, f32[2,4,34,1]{3,2,1,0:T(8,128)S(1)}, u32[]{:S(2)}, u32[]{:S(2)}) collective-permute-start(f32[2,4,34,1]{3,2,1,0:T(8,128)S(1)} %get-tuple-element.671), channel_id=1, source_target_pairs={{1,0},{2,1},{3,2},{0,3},{5,4},{6,5},{7,6},{4,7},{9,8},{10,9},{11,1... | collective-permute-start | bytes 3272 | tf_op jit(solution)/shard_map/while/body/eval_jaxpr/ppermute | solution.py:21
  108.1 8.1 %collective-permute-start.2 = (f32[2,4,34,1]{3,2,1,0:T(8,128)S(1)}, f32[2,4,34,1]{3,2,1,0:T(8,128)S(1)}, u32[]{:S(2)}, u32[]{:S(2)}) collective-permute-start(f32[2,4,34,1]{3,2,1,0:T(8,128)S(1)} %get-tuple-element.670), channel_id=1, source_target_pairs={{0,1},{1,2},{2,3},{3,0},{4,5},{5,6},{6,7},{7,4},{8,9},{9,10},{10,1... | collective-permute-start | bytes 3272 | tf_op jit(solution)/shard_map/while/body/eval_jaxpr/ppermute | solution.py:20
  108.6 8.9 %collective-permute-start.3 = (f32[2,4,34,1]{3,2,1,0:T(8,128)S(1)}, f32[2,4,34,1]{3,2,1,0:T(8,128)S(1)}, u32[]{:S(2)}, u32[]{:S(2)}) collective-permute-start(f32[2,4,34,1]{3,2,1,0:T(8,128)S(1)} %get-tuple-element.671), channel_id=1, source_target_pairs={{1,0},{2,1},{3,2},{0,3},{5,4},{6,5},{7,6},{4,7},{9,8},{10,9},{11,1... | collective-permute-start | bytes 3272 | tf_op jit(solution)/shard_map/while/body/eval_jaxpr/ppermute | solution.py:21
  124.7 8.6 %collective-permute-start.2 = (f32[2,4,34,1]{3,2,1,0:T(8,128)S(1)}, f32[2,4,34,1]{3,2,1,0:T(8,128)S(1)}, u32[]{:S(2)}, u32[]{:S(2)}) collective-permute-start(f32[2,4,34,1]{3,2,1,0:T(8,128)S(1)} %get-tuple-element.670), channel_id=1, source_target_pairs={{0,1},{1,2},{2,3},{3,0},{4,5},{5,6},{6,7},{7,4},{8,9},{9,10},{10,1... | collective-permute-start | bytes 3272 | tf_op jit(solution)/shard_map/while/body/eval_jaxpr/ppermute | solution.py:20
  125.3 8.5 %collective-permute-start.3 = (f32[2,4,34,1]{3,2,1,0:T(8,128)S(1)}, f32[2,4,34,1]{3,2,1,0:T(8,128)S(1)}, u32[]{:S(2)}, u32[]{:S(2)}) collective-permute-start(f32[2,4,34,1]{3,2,1,0:T(8,128)S(1)} %get-tuple-element.671), channel_id=1, source_target_pairs={{1,0},{2,1},{3,2},{0,3},{5,4},{6,5},{7,6},{4,7},{9,8},{10,9},{11,1... | collective-permute-start | bytes 3272 | tf_op jit(solution)/shard_map/while/body/eval_jaxpr/ppermute | solution.py:21
  138.2 7.3 %collective-permute-start.2 = (f32[2,4,34,1]{3,2,1,0:T(8,128)S(1)}, f32[2,4,34,1]{3,2,1,0:T(8,128)S(1)}, u32[]{:S(2)}, u32[]{:S(2)}) collective-permute-start(f32[2,4,34,1]{3,2,1,0:T(8,128)S(1)} %get-tuple-element.670), channel_id=1, source_target_pairs={{0,1},{1,2},{2,3},{3,0},{4,5},{5,6},{6,7},{7,4},{8,9},{9,10},{10,1... | collective-permute-start | bytes 3272 | tf_op jit(solution)/shard_map/while/body/eval_jaxpr/ppermute | solution.py:20
  139.9 7.1 %collective-permute-start.3 = (f32[2,4,34,1]{3,2,1,0:T(8,128)S(1)}, f32[2,4,34,1]{3,2,1,0:T(8,128)S(1)}, u32[]{:S(2)}, u32[]{:S(2)}) collective-permute-start(f32[2,4,34,1]{3,2,1,0:T(8,128)S(1)} %get-tuple-element.671), channel_id=1, source_target_pairs={{1,0},{2,1},{3,2},{0,3},{5,4},{6,5},{7,6},{4,7},{9,8},{10,9},{11,1... | collective-permute-start | bytes 3272 | tf_op jit(solution)/shard_map/while/body/eval_jaxpr/ppermute | solution.py:21
  152.8 7.3 %collective-permute-start.2 = (f32[2,4,34,1]{3,2,1,0:T(8,128)S(1)}, f32[2,4,34,1]{3,2,1,0:T(8,128)S(1)}, u32[]{:S(2)}, u32[]{:S(2)}) collective-permute-start(f32[2,4,34,1]{3,2,1,0:T(8,128)S(1)} %get-tuple-element.670), channel_id=1, source_target_pairs={{0,1},{1,2},{2,3},{3,0},{4,5},{5,6},{6,7},{7,4},{8,9},{9,10},{10,1... | collective-permute-start | bytes 3272 | tf_op jit(solution)/shard_map/while/body/eval_jaxpr/ppermute | solution.py:20
  153.5 7.1 %collective-permute-start.3 = (f32[2,4,34,1]{3,2,1,0:T(8,128)S(1)}, f32[2,4,34,1]{3,2,1,0:T(8,128)S(1)}, u32[]{:S(2)}, u32[]{:S(2)}) collective-permute-start(f32[2,4,34,1]{3,2,1,0:T(8,128)S(1)} %get-tuple-element.671), channel_id=1, source_target_pairs={{1,0},{2,1},{3,2},{0,3},{5,4},{6,5},{7,6},{4,7},{9,8},{10,9},{11,1... | collective-permute-start | bytes 3272 | tf_op jit(solution)/shard_map/while/body/eval_jaxpr/ppermute | solution.py:21
  164.9 7.3 %collective-permute-start.2 = (f32[2,4,34,1]{3,2,1,0:T(8,128)S(1)}, f32[2,4,34,1]{3,2,1,0:T(8,128)S(1)}, u32[]{:S(2)}, u32[]{:S(2)}) collective-permute-start(f32[2,4,34,1]{3,2,1,0:T(8,128)S(1)} %get-tuple-element.670), channel_id=1, source_target_pairs={{0,1},{1,2},{2,3},{3,0},{4,5},{5,6},{6,7},{7,4},{8,9},{9,10},{10,1... | collective-permute-start | bytes 3272 | tf_op jit(solution)/shard_map/while/body/eval_jaxpr/ppermute | solution.py:20
  166.0 7.1 %collective-permute-start.3 = (f32[2,4,34,1]{3,2,1,0:T(8,128)S(1)}, f32[2,4,34,1]{3,2,1,0:T(8,128)S(1)}, u32[]{:S(2)}, u32[]{:S(2)}) collective-permute-start(f32[2,4,34,1]{3,2,1,0:T(8,128)S(1)} %get-tuple-element.671), channel_id=1, source_target_pairs={{1,0},{2,1},{3,2},{0,3},{5,4},{6,5},{7,6},{4,7},{9,8},{10,9},{11,1... | collective-permute-start | bytes 3272 | tf_op jit(solution)/shard_map/while/body/eval_jaxpr/ppermute | solution.py:21
  178.7 8.8 %collective-permute-start.2 = (f32[2,4,34,1]{3,2,1,0:T(8,128)S(1)}, f32[2,4,34,1]{3,2,1,0:T(8,128)S(1)}, u32[]{:S(2)}, u32[]{:S(2)}) collective-permute-start(f32[2,4,34,1]{3,2,1,0:T(8,128)S(1)} %get-tuple-element.670), channel_id=1, source_target_pairs={{0,1},{1,2},{2,3},{3,0},{4,5},{5,6},{6,7},{7,4},{8,9},{9,10},{10,1... | collective-permute-start | bytes 3272 | tf_op jit(solution)/shard_map/while/body/eval_jaxpr/ppermute | solution.py:20
  180.4 7.9 %collective-permute-start.3 = (f32[2,4,34,1]{3,2,1,0:T(8,128)S(1)}, f32[2,4,34,1]{3,2,1,0:T(8,128)S(1)}, u32[]{:S(2)}, u32[]{:S(2)}) collective-permute-start(f32[2,4,34,1]{3,2,1,0:T(8,128)S(1)} %get-tuple-element.671), channel_id=1, source_target_pairs={{1,0},{2,1},{3,2},{0,3},{5,4},{6,5},{7,6},{4,7},{9,8},{10,9},{11,1... | collective-permute-start | bytes 3272 | tf_op jit(solution)/shard_map/while/body/eval_jaxpr/ppermute | solution.py:21
  192.6 7.3 %collective-permute-start.2 = (f32[2,4,34,1]{3,2,1,0:T(8,128)S(1)}, f32[2,4,34,1]{3,2,1,0:T(8,128)S(1)}, u32[]{:S(2)}, u32[]{:S(2)}) collective-permute-start(f32[2,4,34,1]{3,2,1,0:T(8,128)S(1)} %get-tuple-element.670), channel_id=1, source_target_pairs={{0,1},{1,2},{2,3},{3,0},{4,5},{5,6},{6,7},{7,4},{8,9},{9,10},{10,1... | collective-permute-start | bytes 3272 | tf_op jit(solution)/shard_map/while/body/eval_jaxpr/ppermute | solution.py:20
  194.5 7.0 %collective-permute-start.3 = (f32[2,4,34,1]{3,2,1,0:T(8,128)S(1)}, f32[2,4,34,1]{3,2,1,0:T(8,128)S(1)}, u32[]{:S(2)}, u32[]{:S(2)}) collective-permute-start(f32[2,4,34,1]{3,2,1,0:T(8,128)S(1)} %get-tuple-element.671), channel_id=1, source_target_pairs={{1,0},{2,1},{3,2},{0,3},{5,4},{6,5},{7,6},{4,7},{9,8},{10,9},{11,1... | collective-permute-start | bytes 3272 | tf_op jit(solution)/shard_map/while/body/eval_jaxpr/ppermute | solution.py:21
  209.2 6.4 %collective-permute-start.10 = (f32[4,34,1]{2,1,0:T(8,128)S(1)}, f32[4,34,1]{2,1,0:T(8,128)S(1)}, u32[]{:S(2)}, u32[]{:S(2)}) collective-permute-start(f32[4,34,1]{2,1,0:T(8,128)S(1)} %get-tuple-element.698), channel_id=1, source_target_pairs={{0,1},{1,2},{2,3},{3,0},{4,5},{5,6},{6,7},{7,4},{8,9},{9,10},{10,1... | collective-permute-start | bytes 1640 | tf_op jit(solution)/shard_map/while/body/eval_jaxpr/ppermute | solution.py:20
  220.7 6.4 %collective-permute-start.10 = (f32[4,34,1]{2,1,0:T(8,128)S(1)}, f32[4,34,1]{2,1,0:T(8,128)S(1)}, u32[]{:S(2)}, u32[]{:S(2)}) collective-permute-start(f32[4,34,1]{2,1,0:T(8,128)S(1)} %get-tuple-element.698), channel_id=1, source_target_pairs={{0,1},{1,2},{2,3},{3,0},{4,5},{5,6},{6,7},{7,4},{8,9},{9,10},{10,1... | collective-permute-start | bytes 1640 | tf_op jit(solution)/shard_map/while/body/eval_jaxpr/ppermute | solution.py:20
  243.6 7.5 %collective-permute-start.10 = (f32[4,34,1]{2,1,0:T(8,128)S(1)}, f32[4,34,1]{2,1,0:T(8,128)S(1)}, u32[]{:S(2)}, u32[]{:S(2)}) collective-permute-start(f32[4,34,1]{2,1,0:T(8,128)S(1)} %get-tuple-element.698), channel_id=1, source_target_pairs={{0,1},{1,2},{2,3},{3,0},{4,5},{5,6},{6,7},{7,4},{8,9},{9,10},{10,1... | collective-permute-start | bytes 1640 | tf_op jit(solution)/shard_map/while/body/eval_jaxpr/ppermute | solution.py:20
  244.9 6.7 %collective-permute-start.11 = (f32[4,34,1]{2,1,0:T(8,128)S(1)}, f32[4,34,1]{2,1,0:T(8,128)S(1)}, u32[]{:S(2)}, u32[]{:S(2)}) collective-permute-start(f32[4,34,1]{2,1,0:T(8,128)S(1)} %get-tuple-element.699), channel_id=1, source_target_pairs={{1,0},{2,1},{3,2},{0,3},{5,4},{6,5},{7,6},{4,7},{9,8},{10,9},{11,1... | collective-permute-start | bytes 1640 | tf_op jit(solution)/shard_map/while/body/eval_jaxpr/ppermute | solution.py:21
  256.4 6.5 %collective-permute-start.10 = (f32[4,34,1]{2,1,0:T(8,128)S(1)}, f32[4,34,1]{2,1,0:T(8,128)S(1)}, u32[]{:S(2)}, u32[]{:S(2)}) collective-permute-start(f32[4,34,1]{2,1,0:T(8,128)S(1)} %get-tuple-element.698), channel_id=1, source_target_pairs={{0,1},{1,2},{2,3},{3,0},{4,5},{5,6},{6,7},{7,4},{8,9},{9,10},{10,1... | collective-permute-start | bytes 1640 | tf_op jit(solution)/shard_map/while/body/eval_jaxpr/ppermute | solution.py:20
  291.7 7.1 %collective-permute-start.10 = (f32[4,34,1]{2,1,0:T(8,128)S(1)}, f32[4,34,1]{2,1,0:T(8,128)S(1)}, u32[]{:S(2)}, u32[]{:S(2)}) collective-permute-start(f32[4,34,1]{2,1,0:T(8,128)S(1)} %get-tuple-element.698), channel_id=1, source_target_pairs={{0,1},{1,2},{2,3},{3,0},{4,5},{5,6},{6,7},{7,4},{8,9},{9,10},{10,1... | collective-permute-start | bytes 1640 | tf_op jit(solution)/shard_map/while/body/eval_jaxpr/ppermute | solution.py:20
  303.7 6.4 %collective-permute-start.10 = (f32[4,34,1]{2,1,0:T(8,128)S(1)}, f32[4,34,1]{2,1,0:T(8,128)S(1)}, u32[]{:S(2)}, u32[]{:S(2)}) collective-permute-start(f32[4,34,1]{2,1,0:T(8,128)S(1)} %get-tuple-element.698), channel_id=1, source_target_pairs={{0,1},{1,2},{2,3},{3,0},{4,5},{5,6},{6,7},{7,4},{8,9},{9,10},{10,1... | collective-permute-start | bytes 1640 | tf_op jit(solution)/shard_map/while/body/eval_jaxpr/ppermute | solution.py:20
  326.4 7.7 %collective-permute-start.10 = (f32[4,34,1]{2,1,0:T(8,128)S(1)}, f32[4,34,1]{2,1,0:T(8,128)S(1)}, u32[]{:S(2)}, u32[]{:S(2)}) collective-permute-start(f32[4,34,1]{2,1,0:T(8,128)S(1)} %get-tuple-element.698), channel_id=1, source_target_pairs={{0,1},{1,2},{2,3},{3,0},{4,5},{5,6},{6,7},{7,4},{8,9},{9,10},{10,1... | collective-permute-start | bytes 1640 | tf_op jit(solution)/shard_map/while/body/eval_jaxpr/ppermute | solution.py:20
  327.8 7.0 %collective-permute-start.11 = (f32[4,34,1]{2,1,0:T(8,128)S(1)}, f32[4,34,1]{2,1,0:T(8,128)S(1)}, u32[]{:S(2)}, u32[]{:S(2)}) collective-permute-start(f32[4,34,1]{2,1,0:T(8,128)S(1)} %get-tuple-element.699), channel_id=1, source_target_pairs={{1,0},{2,1},{3,2},{0,3},{5,4},{6,5},{7,6},{4,7},{9,8},{10,9},{11,1... | collective-permute-start | bytes 1640 | tf_op jit(solution)/shard_map/while/body/eval_jaxpr/ppermute | solution.py:21
  340.0 6.4 %collective-permute-start.10 = (f32[4,34,1]{2,1,0:T(8,128)S(1)}, f32[4,34,1]{2,1,0:T(8,128)S(1)}, u32[]{:S(2)}, u32[]{:S(2)}) collective-permute-start(f32[4,34,1]{2,1,0:T(8,128)S(1)} %get-tuple-element.698), channel_id=1, source_target_pairs={{0,1},{1,2},{2,3},{3,0},{4,5},{5,6},{6,7},{7,4},{8,9},{9,10},{10,1... | collective-permute-start | bytes 1640 | tf_op jit(solution)/shard_map/while/body/eval_jaxpr/ppermute | solution.py:20
  374.6 7.6 %collective-permute-start.10 = (f32[4,34,1]{2,1,0:T(8,128)S(1)}, f32[4,34,1]{2,1,0:T(8,128)S(1)}, u32[]{:S(2)}, u32[]{:S(2)}) collective-permute-start(f32[4,34,1]{2,1,0:T(8,128)S(1)} %get-tuple-element.698), channel_id=1, source_target_pairs={{0,1},{1,2},{2,3},{3,0},{4,5},{5,6},{6,7},{7,4},{8,9},{9,10},{10,1... | collective-permute-start | bytes 1640 | tf_op jit(solution)/shard_map/while/body/eval_jaxpr/ppermute | solution.py:20
  375.7 6.7 %collective-permute-start.11 = (f32[4,34,1]{2,1,0:T(8,128)S(1)}, f32[4,34,1]{2,1,0:T(8,128)S(1)}, u32[]{:S(2)}, u32[]{:S(2)}) collective-permute-start(f32[4,34,1]{2,1,0:T(8,128)S(1)} %get-tuple-element.699), channel_id=1, source_target_pairs={{1,0},{2,1},{3,2},{0,3},{5,4},{6,5},{7,6},{4,7},{9,8},{10,9},{11,1... | collective-permute-start | bytes 1640 | tf_op jit(solution)/shard_map/while/body/eval_jaxpr/ppermute | solution.py:21
  423.6 6.5 %collective-permute-start.6 = (f32[4,34,1]{2,1,0:T(8,128)S(1)}, f32[4,34,1]{2,1,0:T(8,128)S(1)}, u32[]{:S(2)}, u32[]{:S(2)}) collective-permute-start(f32[4,34,1]{2,1,0:T(8,128)S(1)} %get-tuple-element.685), channel_id=1, source_target_pairs={{0,1},{1,2},{2,3},{3,0},{4,5},{5,6},{6,7},{7,4},{8,9},{9,10},{10,1... | collective-permute-start | bytes 1640 | tf_op jit(solution)/shard_map/while/body/eval_jaxpr/ppermute | solution.py:20
  434.4 6.4 %collective-permute-start.6 = (f32[4,34,1]{2,1,0:T(8,128)S(1)}, f32[4,34,1]{2,1,0:T(8,128)S(1)}, u32[]{:S(2)}, u32[]{:S(2)}) collective-permute-start(f32[4,34,1]{2,1,0:T(8,128)S(1)} %get-tuple-element.685), channel_id=1, source_target_pairs={{0,1},{1,2},{2,3},{3,0},{4,5},{5,6},{6,7},{7,4},{8,9},{9,10},{10,1... | collective-permute-start | bytes 1640 | tf_op jit(solution)/shard_map/while/body/eval_jaxpr/ppermute | solution.py:20
  448.1 6.5 %collective-permute-start.7 = (f32[4,34,1]{2,1,0:T(8,128)S(1)}, f32[4,34,1]{2,1,0:T(8,128)S(1)}, u32[]{:S(2)}, u32[]{:S(2)}) collective-permute-start(f32[4,34,1]{2,1,0:T(8,128)S(1)} %get-tuple-element.686), channel_id=1, source_target_pairs={{1,0},{2,1},{3,2},{0,3},{5,4},{6,5},{7,6},{4,7},{9,8},{10,9},{11,1... | collective-permute-start | bytes 1640 | tf_op jit(solution)/shard_map/while/body/eval_jaxpr/ppermute | solution.py:21
  458.6 6.9 %collective-permute-start.6 = (f32[4,34,1]{2,1,0:T(8,128)S(1)}, f32[4,34,1]{2,1,0:T(8,128)S(1)}, u32[]{:S(2)}, u32[]{:S(2)}) collective-permute-start(f32[4,34,1]{2,1,0:T(8,128)S(1)} %get-tuple-element.685), channel_id=1, source_target_pairs={{0,1},{1,2},{2,3},{3,0},{4,5},{5,6},{6,7},{7,4},{8,9},{9,10},{10,1... | collective-permute-start | bytes 1640 | tf_op jit(solution)/shard_map/while/body/eval_jaxpr/ppermute | solution.py:20
  494.0 6.4 %collective-permute-start.6 = (f32[4,34,1]{2,1,0:T(8,128)S(1)}, f32[4,34,1]{2,1,0:T(8,128)S(1)}, u32[]{:S(2)}, u32[]{:S(2)}) collective-permute-start(f32[4,34,1]{2,1,0:T(8,128)S(1)} %get-tuple-element.685), channel_id=1, source_target_pairs={{0,1},{1,2},{2,3},{3,0},{4,5},{5,6},{6,7},{7,4},{8,9},{9,10},{10,1... | collective-permute-start | bytes 1640 | tf_op jit(solution)/shard_map/while/body/eval_jaxpr/ppermute | solution.py:20
  517.1 6.4 %collective-permute-start.6 = (f32[4,34,1]{2,1,0:T(8,128)S(1)}, f32[4,34,1]{2,1,0:T(8,128)S(1)}, u32[]{:S(2)}, u32[]{:S(2)}) collective-permute-start(f32[4,34,1]{2,1,0:T(8,128)S(1)} %get-tuple-element.685), channel_id=1, source_target_pairs={{0,1},{1,2},{2,3},{3,0},{4,5},{5,6},{6,7},{7,4},{8,9},{9,10},{10,1... | collective-permute-start | bytes 1640 | tf_op jit(solution)/shard_map/while/body/eval_jaxpr/ppermute | solution.py:20
  540.1 6.4 %collective-permute-start.6 = (f32[4,34,1]{2,1,0:T(8,128)S(1)}, f32[4,34,1]{2,1,0:T(8,128)S(1)}, u32[]{:S(2)}, u32[]{:S(2)}) collective-permute-start(f32[4,34,1]{2,1,0:T(8,128)S(1)} %get-tuple-element.685), channel_id=1, source_target_pairs={{0,1},{1,2},{2,3},{3,0},{4,5},{5,6},{6,7},{7,4},{8,9},{9,10},{10,1... | collective-permute-start | bytes 1640 | tf_op jit(solution)/shard_map/while/body/eval_jaxpr/ppermute | solution.py:20
  563.1 6.4 %collective-permute-start.6 = (f32[4,34,1]{2,1,0:T(8,128)S(1)}, f32[4,34,1]{2,1,0:T(8,128)S(1)}, u32[]{:S(2)}, u32[]{:S(2)}) collective-permute-start(f32[4,34,1]{2,1,0:T(8,128)S(1)} %get-tuple-element.685), channel_id=1, source_target_pairs={{0,1},{1,2},{2,3},{3,0},{4,5},{5,6},{6,7},{7,4},{8,9},{9,10},{10,1... | collective-permute-start | bytes 1640 | tf_op jit(solution)/shard_map/while/body/eval_jaxpr/ppermute | solution.py:20
  (140 other events, 798.1 us)
where the time goes:
time: 593 us
  waiting for transfers between devices  280 us (47%)
  starting transfers between devices  279 us (47%)
  other arithmetic  10.7 us (2%)
  blocking collectives  10.1 us (2%)
  local copies, waits for them, and re-layouts  6.83 us (1%)
    ppermute x92, waiting for transfers between devices, extended_2(): before = lax.ppermute(last, axis, up)  186 us
    ppermute x92, starting transfers between devices, extended_2(): after = lax.ppermute(initial, axis, down)  180 us
    ppermute x92, starting transfers between devices, extended_2(): before = lax.ppermute(last, axis, up)  98.8 us
    ppermute x92, waiting for transfers between devices, extended_2(): after = lax.ppermute(initial, axis, down)  94.1 us
  transfers between devices with their start and end apart: 184, of which 165 were waited for; matrix products, arithmetic and copies ran while one was open for 0% of the time, Pallas kernels for 0%

commit v1 on v0

--- a/solution.py
+++ b/solution.py
@@ -3,6 +3,8 @@
 import jax
 import jax.numpy as jnp
 from jax import lax
+from jax.experimental import pallas as pl
+from jax.experimental.pallas import tpu as pltpu
 from jax.sharding import PartitionSpec as P
 
 SEG = 16
@@ -101,9 +103,310 @@
     return (gradient, jnp.stack([adjoint_zero, adjoint_first]))
 
 
+MESH = pl.DeviceIdType.MESH
+TERMS = 2 * SEG
+ROWS = 32
+LANES = 128
+REACH = 32
+DEPTH = 8
+ENERGIES = 16
+X_CK, X_ADJ, X_BITS, X_POT, X_RES, X_GRAD, X_OUT = range(7)
+Z_CK, Z_ADJ, Z_RES = range(3)
+Z_PARTS = ((0, 2), (2, 2), (4, 4))
+PACKS = 8
+
+
+def pick_quarter(lane, parts):
+    low = jnp.where(lane < REACH, parts[0], parts[1])
+    high = jnp.where(lane < 3 * REACH, parts[2], parts[3])
+    return jnp.where(lane < 2 * REACH, low, high)
+
+
+def turn(value, shift):
+    shift = shift % LANES
+    return value if shift == 0 else pltpu.roll(value, shift, 1)
+
+
+def kernel(
+    scal, kron, ck, adj, bits, pot, res, grad_out, adj_out,
+    wck, wadj, wbits, wpot, wres, zsend, zrecv, states, adjs, onsite, signs, rwin, weights,
+    gbuf, gother, gall, obuf, xs, xr, zs, zr, vs, vr,
+):
+    x = lax.axis_index("row")
+    z = lax.axis_index("col")
+    y = lax.axis_index("vec")
+    n_z = lax.axis_size("col")
+    n_y = lax.axis_size("vec")
+    across = {"row": 1 - x}
+    right = {"col": lax.rem(z + 1, n_z)}
+    left = {"col": lax.rem(z + n_z - 1, n_z)}
+    peers = [{"vec": lax.rem(y + d, n_y)} for d in range(1, n_y)]
+
+    barrier = pltpu.get_barrier_semaphore()
+    for device in [across, right, left] + peers:
+        pl.semaphore_signal(barrier, inc=1, device_id=device, device_id_type=MESH)
+    pl.semaphore_wait(barrier, 3 + len(peers))
+
+    def remote(source, target, send, recv, device):
+        copy = pltpu.make_async_remote_copy(
+            src_ref=source, dst_ref=target, send_sem=send, recv_sem=recv,
+            device_id=device, device_id_type=MESH,
+        )
+        copy.start()
+        return copy
+
+    def to_x(source, target, index):
+        return remote(source, target, xs.at[index], xr.at[index], across)
+
+    theirs = pl.ds(2 * (1 - x), 2)
+    mine = pl.ds(2 * x, 2)
+    other = pl.ds(ROWS, ROWS)
+    own = pl.ds(0, ROWS)
+    c_ck = to_x(ck.at[:, :, theirs], wck.at[:, :, :, other], X_CK)
+    c_adj = to_x(adj.at[:, theirs], wadj.at[:, :, other], X_ADJ)
+    c_bits = to_x(bits.at[theirs], wbits.at[:, other], X_BITS)
+    c_pot = to_x(pot, wpot.at[other], X_POT)
+    c_res = to_x(res, wres.at[:, other], X_RES)
+
+    wck[:, :, :, own] = ck[:, :, mine]
+    wadj[:, :, own] = adj[:, mine]
+    wbits[:, own] = bits[mine]
+    wpot[own] = pot[...]
+    wres[:, own] = res[...]
+
+    lane = lax.broadcasted_iota(jnp.int32, (8, LANES), 1)
+
+    def rows(j):
+        return pl.ds(j, 8, stride=8)
+
+    def pack(slot, j, planes):
+        zsend[0, slot, j] = pick_quarter(lane, [turn(p, REACH * (q + 1)) for q, p in enumerate(planes)])
+        zsend[1, slot, j] = pick_quarter(lane, [turn(p, REACH * q) for q, p in enumerate(planes)])
+
+    def unpack(slot, j, q):
+        from_left = turn(zrecv[0, slot, j], LANES - REACH - REACH * q)
+        from_right = turn(zrecv[1, slot, j], LANES - REACH * q)
+        return jnp.where(lane < 2 * REACH, from_right, from_left)
+
+    def to_z(part):
+        first, count = Z_PARTS[part]
+        span = pl.ds(first, count)
+        return [
+            remote(zsend.at[d, span], zrecv.at[d, span], zs.at[d, part], zr.at[d, part], device)
+            for d, device in enumerate((right, left))
+        ]
+
+    c_ck.wait()
+    for j in range(DEPTH):
+        for s in range(2):
+            planes = [wck[s, k, v, rows(j)] for k in range(2) for v in range(2)]
+            pack(s, j, planes)
+            for q, plane in enumerate(planes):
+                states[s * SEG + q // 2, q % 2, j, 0] = plane
+    z_ck = to_z(Z_CK)
+
+    pot_factor = scal[0]
+    twice = scal[1]
+    inv_count = scal[2]
+    c_adj.wait()
+    c_bits.wait()
+    c_pot.wait()
+    for j in range(DEPTH):
+        planes = [wadj[k, v, rows(j)] for k in range(2) for v in range(2)]
+        pack(2, j, planes)
+        for q, plane in enumerate(planes):
+            adjs[TERMS + q // 2, q % 2, j, 0] = plane
+        sign = [(2 * wbits[v, rows(j)] - 1).astype(jnp.float32) * inv_count for v in range(2)]
+        site = wpot[rows(j)].astype(jnp.float32) * pot_factor * twice
+        pack(3, j, [sign[0], sign[1], site, site])
+        signs[0, j, 0] = sign[0]
+        signs[1, j, 0] = sign[1]
+        onsite[j, 0] = site
+    z_adj = to_z(Z_ADJ)
+
+    c_res.wait()
+    for j in range(DEPTH):
+        for p in range(4):
+            planes = [wres[4 * p + q, rows(j)] for q in range(4)]
+            pack(4 + p, j, planes)
+            for q, plane in enumerate(planes):
+                rwin[j, 0, 4 * p + q] = plane
+    z_res = to_z(Z_RES)
+
+    def settle(copies):
+        for copy in copies:
+            copy.wait()
+
+    settle(z_ck)
+    for j in range(DEPTH):
+        for s in range(2):
+            for q in range(4):
+                states[s * SEG + q // 2, q % 2, j, 1] = unpack(s, j, q)
+    settle(z_adj)
+    for j in range(DEPTH):
+        for q in range(4):
+            adjs[TERMS + q // 2, q % 2, j, 1] = unpack(2, j, q)
+        signs[0, j, 1] = unpack(3, j, 0)
+        signs[1, j, 1] = unpack(3, j, 1)
+        onsite[j, 1] = unpack(3, j, 2)
+
+    first_lane = lane == 0
+    last_lane = lane == LANES - 1
+
+    def beside(ref, t, v, j):
+        here = [ref[t, v, j, c] for c in range(2)]
+        back = [pltpu.roll(w, 1, 1) for w in here]
+        ahead = [pltpu.roll(w, LANES - 1, 1) for w in here]
+        sums = []
+        for c in range(2):
+            before = jnp.where(first_lane, back[1 - c], back[c])
+            after = jnp.where(last_lane, ahead[1 - c], ahead[c])
+            if j == 0:
+                above = pltpu.roll(ref[t, v, DEPTH - 1, c], 1, 0)
+            else:
+                above = ref[t, v, j - 1, c]
+            if j == DEPTH - 1:
+                below = pltpu.roll(ref[t, v, 0, c], 7, 0)
+            else:
+                below = ref[t, v, j + 1, c]
+            sums.append((above + below) + (before + after))
+        return here, sums
+
+    def forward(k, carry):
+        for s in range(2):
+            t = s * SEG + k
+            for v in range(2):
+                for j in range(DEPTH):
+                    here, sums = beside(states, t - 1, v, j)
+                    for c in range(2):
+                        states[t, v, j, c] = (onsite[j, c] * here[c] - twice * sums[c]) - states[t - 2, v, j, c]
+        return carry
+
+    lax.fori_loop(2, SEG, forward, 0)
+
+    def halves(value):
+        high = value.astype(jnp.bfloat16)
+        return high, (value - high.astype(jnp.float32)).astype(jnp.bfloat16)
+
+    kron_high, kron_low = halves(kron[...])
+
+    def weigh(c):
+        for j in range(DEPTH):
+            high, low = halves(rwin[j, c].reshape(ENERGIES * 8, LANES))
+            dot = lambda a, b: jnp.dot(a, b, preferred_element_type=jnp.float32)
+            total = dot(kron_high, high) + (dot(kron_high, low) + dot(kron_low, high))
+            weights[j, c] = total.reshape(TERMS, 8, LANES)
+
+    weigh(0)
+    settle(z_res)
+    for j in range(DEPTH):
+        for p in range(4):
+            for q in range(4):
+                rwin[j, 1, 4 * p + q] = unpack(4 + p, j, q)
+    weigh(1)
+
+    def adjoint(i, sums_in):
+        t = TERMS - 1 - i
+        grads = list(sums_in)
+        for v in range(2):
+            for j in range(DEPTH):
+                here, sums = beside(adjs, t + 1, v, j)
+                grads[j] = grads[j] + here[0] * states[t, v, j, 0]
+                for c in range(2):
+                    source = weights[j, c, t] * signs[v, j, c]
+                    adjs[t, v, j, c] = (source + onsite[j, c] * here[c]) - (twice * sums[c] + adjs[t + 2, v, j, c])
+        return tuple(grads)
+
+    zero = jnp.zeros((8, LANES), jnp.float32)
+    grads = lax.fori_loop(0, TERMS, adjoint, (zero,) * DEPTH)
+
+    for j in range(DEPTH):
+        gbuf[rows(j)] = grads[j]
+        for k in range(2):
+            for v in range(2):
+                obuf[k, v, rows(j)] = adjs[k, v, j, 0]
+    c_grad = to_x(gbuf.at[other], gother, X_GRAD)
+    c_out = to_x(obuf.at[:, :, other], adj_out.at[:, mine], X_OUT)
+    adj_out[:, mine] = obuf[:, :, own]
+    c_grad.wait()
+    gall[y] = gbuf[own] + gother[...]
+    shares = [
+        remote(gall.at[y], gall.at[y], vs.at[d], vr.at[d], device) for d, device in enumerate(peers)
+    ]
+    settle(shares)
+    total = gall[0]
+    for d in range(1, n_y):
+        total = total + gall[d]
+    grad_out[...] = total * twice
+    c_out.wait()
+
+
+def windowed(
+    checkpoints,
+    adjoints_in,
+    vector_bits,
+    potential_int,
+    pot_scale,
+    energies,
+    residual,
+    first_segment,
+):
+    n_y = lax.axis_size("vec")
+    pot_factor = pot_scale[0]
+    twice = 2.0 / (4.5 + QMAX * pot_factor)
+    coefficients = window_coefs(first_segment, energies)
+    inv_count = 1.0 / (n_y * vector_bits.shape[0])
+    scal = jnp.stack([pot_factor, twice, jnp.float32(inv_count)])
+    spread = coefficients[:, None, :, None] * jnp.eye(8, dtype=jnp.float32)[None, :, None, :]
+    spread = spread.reshape(TERMS * 8, ENERGIES * 8)
+    kron = spread
+    f32, i32 = jnp.float32, jnp.int32
+    vmem = pl.BlockSpec(memory_space=pltpu.VMEM)
+    tile = (8, LANES)
+    gradient, adjoint_out = pl.pallas_call(
+        kernel,
+        out_shape=(
+            jax.ShapeDtypeStruct(potential_int.shape, f32),
+            jax.ShapeDtypeStruct(adjoints_in.shape, f32),
+        ),
+        in_specs=[pl.BlockSpec(memory_space=pltpu.SMEM)] + [vmem] * 6,
+        out_specs=(vmem, vmem),
+        scratch_shapes=[
+            pltpu.VMEM((2, 2, 2, 2 * ROWS, LANES), f32),
+            pltpu.VMEM((2, 2, 2 * ROWS, LANES), f32),
+            pltpu.VMEM((2, 2 * ROWS, LANES), i32),
+            pltpu.VMEM((2 * ROWS, LANES), i32),
+            pltpu.VMEM((ENERGIES, 2 * ROWS, LANES), f32),
+            pltpu.VMEM((2, PACKS, DEPTH) + tile, f32),
+            pltpu.VMEM((2, PACKS, DEPTH) + tile, f32),
+            pltpu.VMEM((TERMS, 2, DEPTH, 2) + tile, f32),
+            pltpu.VMEM((TERMS + 2, 2, DEPTH, 2) + tile, f32),
+            pltpu.VMEM((DEPTH, 2) + tile, f32),
+            pltpu.VMEM((2, DEPTH, 2) + tile, f32),
+            pltpu.VMEM((DEPTH, 2, ENERGIES) + tile, f32),
+            pltpu.VMEM((DEPTH, 2, TERMS) + tile, f32),
+            pltpu.VMEM((2 * ROWS, LANES), f32),
+            pltpu.VMEM((ROWS, LANES), f32),
+            pltpu.VMEM((n_y, ROWS, LANES), f32),
+            pltpu.VMEM((2, 2, 2 * ROWS, LANES), f32),
+            pltpu.SemaphoreType.DMA((7,)),
+            pltpu.SemaphoreType.DMA((7,)),
+            pltpu.SemaphoreType.DMA((2, 3)),
+            pltpu.SemaphoreType.DMA((2, 3)),
+            pltpu.SemaphoreType.DMA((n_y - 1,)),
+            pltpu.SemaphoreType.DMA((n_y - 1,)),
+        ],
+        compiler_params=pltpu.CompilerParams(
+            collective_id=0, has_side_effects=True, vmem_limit_bytes=40 * 1024 * 1024
+        ),
+    )(scal, kron, checkpoints, adjoints_in, vector_bits, potential_int, residual)
+    return gradient, adjoint_out
+
+
 def solution(mesh):
+    fits = mesh.shape["row"] == 2 and mesh.shape["col"] > 2
     return jax.shard_map(
-        per_device,
+        windowed if fits else per_device,
         mesh=mesh,
         in_specs=(
             P(None, None, "vec", "row", "col"),

time: 593 us -> 90.6 us (0.15)
  waiting for transfers between devices: 280 us -> 0 us
  starting transfers between devices: 279 us -> 0 us
  Pallas kernels: 0 us -> 84.8 us
  blocking collectives: 10.1 us -> 0 us
  other arithmetic: 10.7 us -> 1.2 us
    ppermute x184 -> x0, waiting for transfers between devices: 280 us -> none  [the longest x92 186 us: extended_2(): before = lax.ppermute(last, axis, up)]
    ppermute x184 -> x0, starting transfers between devices: 279 us -> none  [the longest x92 180 us: extended_2(): after = lax.ppermute(initial, axis, down)]
    pallas_call x0 -> x1, Pallas kernels: none -> 84.8 us  [windowed(): pl.pallas_call(kernel, out_shape=(jax.ShapeDtypeStruct(potential_int.shap...]
    psum x1 -> x0, blocking collectives: 10.1 us -> none  [per_device(): gradient = lax.psum(accum_grad, 'vec') * (2.0 * inv_span)]
  transfers between devices with their start and end apart: 184 -> 0, of which waited for: 165 -> 0; matrix products, arithmetic and copies ran while one was open for 0% -> 0% of each run, Pallas kernels for 0% -> 0%
where the time goes in v1:
time: 90.6 us; the launch traced here: 90.4 us
  Pallas kernels  84.8 us (94%)
  local copies, waits for them, and re-layouts  2.4 us (3%)
  between operations  2.07 us (2%)
  other arithmetic  1.2 us (1%)
    pallas_call x1, Pallas kernels, windowed(): pl.pallas_call(kernel, out_shape=(jax.ShapeDtypeStruct(potential_int.shap...  84.8 us

profile of v1, /device:TPU:0, one launch (start us, length us, event | category | flops | bytes accessed | tf_op | source)
XLA Modules:
  0.0 90.4 jit_solution(5338487879305862466)
XLA Ops:
  1.3 0.7 sine_multiply_fusion
  2.1 0.1 multiply_divide_fusion
  2.2 0.1 copy.10
  2.3 0.0 copy-start
  2.3 0.0 copy-start.1
  2.3 0.0 copy-start.2
  2.3 0.0 copy-start.3
  2.3 0.0 copy-start.4
  2.3 0.2 broadcast_multiply_fusion
  2.6 1.0 %mul.103.kron = f32[256,128]{1,0:T(8,128)S(1)} reshape(f32[32,8,16,8]{3,2,1,0:T(8,128)S(1)} %broadcast_multiply_fusion) | data formatting | bytes 262144 | tf_op jit(solution)/shard_map/mul | solution.py:360
  4.3 0.1 pad_maximum_fusion.scal
  4.4 0.0 copy-done
  4.4 0.0 copy-done.1
  4.4 0.0 copy-done.2
  4.4 0.0 copy-done.3
  4.4 0.0 copy-done.4
  4.4 84.8 %shard_map.95 = (f32[32,128]{1,0:T(8,128)S(1)}, f32[2,4,32,128]{3,2,1,0:T(8,128)S(1)}) custom-call(f32[3]{0:T(128)S(1)} %pad_maximum_fusion.scal, f32[256,128]{1,0:T(8,128)S(1)} %mul.103.kron, f32[2,2,4,32,128]{4,3,2,1,0:T(8,128)S(1)} %copy-done, f32[2,4,32,128]{3,2,1,0:T(8,128)S(1)} %copy-done.2, s32[4,32,128]{2,1,0:T(8,128)S(1)} %copy-done.3, ...), custom_call_target="tpu_custom_call" | custom-call | tf_op jit(solution)/shard_map/pallas_call | solution.py:366
  89.2 0.6 copy.15
  89.8 0.7 copy.16
  (3 shorter events, 0.1 us)
Async XLA Ops:
  2.3 2.1 %copy-start = (f32[2,2,4,32,128]{4,3,2,1,0:T(8,128)S(1)}, f32[2,2,4,32,128]{4,3,2,1,0:T(8,128)}, u32[]{:S(2)}) copy-start(f32[2,2,4,32,128]{4,3,2,1,0:T(8,128)} %ck.1) | copy-start | bytes 786436
  2.3 2.1 %copy-start.1 = (f32[16,32,128]{2,1,0:T(8,128)S(1)}, f32[16,32,128]{2,1,0:T(8,128)}, u32[]{:S(2)}) copy-start(f32[16,32,128]{2,1,0:T(8,128)} %res.1) | copy-start | bytes 786436
  2.3 2.1 %copy-start.2 = (f32[2,4,32,128]{3,2,1,0:T(8,128)S(1)}, f32[2,4,32,128]{3,2,1,0:T(8,128)}, u32[]{:S(2)}) copy-start(f32[2,4,32,128]{3,2,1,0:T(8,128)} %adj.1) | copy-start | bytes 393220
  2.3 2.1 %copy-start.3 = (s32[4,32,128]{2,1,0:T(8,128)S(1)}, s32[4,32,128]{2,1,0:T(8,128)}, u32[]{:S(2)}) copy-start(s32[4,32,128]{2,1,0:T(8,128)} %bits.1) | copy-start | bytes 196612
  2.3 2.1 %copy-start.4 = (s32[32,128]{1,0:T(8,128)S(1)}, s32[32,128]{1,0:T(8,128)}, u32[]{:S(2)}) copy-start(s32[32,128]{1,0:T(8,128)} %pot.1) | copy-start | bytes 49156

commit v2 on v1

--- a/solution.py
+++ b/solution.py
@@ -128,8 +128,8 @@
 
 
 def kernel(
-    scal, kron, ck, adj, bits, pot, res, grad_out, adj_out,
-    wck, wadj, wbits, wpot, wres, zsend, zrecv, states, adjs, onsite, signs, rwin, weights,
+    scal, coefs, ck, adj, bits, pot, res, grad_out, adj_out,
+    wck, wadj, wbits, wpot, wres, zsend, zrecv, states, even, odd, adj_even, adj_odd, onsite, signs, rwin, weights,
     gbuf, gother, gall, obuf, xs, xr, zs, zr, vs, vr,
 ):
     x = lax.axis_index("row")
@@ -202,7 +202,8 @@
             planes = [wck[s, k, v, rows(j)] for k in range(2) for v in range(2)]
             pack(s, j, planes)
             for q, plane in enumerate(planes):
-                states[s * SEG + q // 2, q % 2, j, 0] = plane
+                states[s * SEG + q // 2, q % 2, j] = plane
+                (even, odd)[q // 2][s, q % 2, j, 0] = plane
     z_ck = to_z(Z_CK)
 
     pot_factor = scal[0]
@@ -215,7 +216,7 @@
         planes = [wadj[k, v, rows(j)] for k in range(2) for v in range(2)]
         pack(2, j, planes)
         for q, plane in enumerate(planes):
-            adjs[TERMS + q // 2, q % 2, j, 0] = plane
+            (adj_even, adj_odd)[q // 2][q % 2, j, 0] = plane
         sign = [(2 * wbits[v, rows(j)] - 1).astype(jnp.float32) * inv_count for v in range(2)]
         site = wpot[rows(j)].astype(jnp.float32) * pot_factor * twice
         pack(3, j, [sign[0], sign[1], site, site])
@@ -241,11 +242,11 @@
     for j in range(DEPTH):
         for s in range(2):
             for q in range(4):
-                states[s * SEG + q // 2, q % 2, j, 1] = unpack(s, j, q)
+                (even, odd)[q // 2][s, q % 2, j, 1] = unpack(s, j, q)
     settle(z_adj)
     for j in range(DEPTH):
         for q in range(4):
-            adjs[TERMS + q // 2, q % 2, j, 1] = unpack(2, j, q)
+            (adj_even, adj_odd)[q // 2][q % 2, j, 1] = unpack(2, j, q)
         signs[0, j, 1] = unpack(3, j, 0)
         signs[1, j, 1] = unpack(3, j, 1)
         onsite[j, 1] = unpack(3, j, 2)
@@ -253,8 +254,8 @@
     first_lane = lane == 0
     last_lane = lane == LANES - 1
 
-    def beside(ref, t, v, j):
-        here = [ref[t, v, j, c] for c in range(2)]
+    def beside(ref, v, j):
+        here = [ref[v, j, c] for c in range(2)]
         back = [pltpu.roll(w, 1, 1) for w in here]
         ahead = [pltpu.roll(w, LANES - 1, 1) for w in here]
         sums = []
@@ -262,33 +263,50 @@
             before = jnp.where(first_lane, back[1 - c], back[c])
             after = jnp.where(last_lane, ahead[1 - c], ahead[c])
             if j == 0:
-                above = pltpu.roll(ref[t, v, DEPTH - 1, c], 1, 0)
+                above = pltpu.roll(ref[v, DEPTH - 1, c], 1, 0)
             else:
-                above = ref[t, v, j - 1, c]
+                above = ref[v, j - 1, c]
             if j == DEPTH - 1:
-                below = pltpu.roll(ref[t, v, 0, c], 7, 0)
+                below = pltpu.roll(ref[v, 0, c], 7, 0)
             else:
-                below = ref[t, v, j + 1, c]
+                below = ref[v, j + 1, c]
             sums.append((above + below) + (before + after))
         return here, sums
 
-    def forward(k, carry):
-        for s in range(2):
-            t = s * SEG + k
-            for v in range(2):
-                for j in range(DEPTH):
-                    here, sums = beside(states, t - 1, v, j)
-                    for c in range(2):
-                        states[t, v, j, c] = (onsite[j, c] * here[c] - twice * sums[c]) - states[t - 2, v, j, c]
+    def forward(half, carry):
+        for step in range(2):
+            now, then = (odd, even) if step == 0 else (even, odd)
+            k = 2 + 2 * half + step
+            for s in range(2):
+                for v in range(2):
+                    for j in range(DEPTH):
+                        here, sums = beside(now.at[s], v, j)
+                        for c in range(2):
+                            value = (onsite[j, c] * here[c] - twice * sums[c]) - then[s, v, j, c]
+                            then[s, v, j, c] = value
+                            if c == 0:
+                                states[s * SEG + k, v, j] = value
         return carry
 
-    lax.fori_loop(2, SEG, forward, 0)
+    lax.fori_loop(0, SEG // 2 - 1, forward, 0)
 
     def halves(value):
         high = value.astype(jnp.bfloat16)
         return high, (value - high.astype(jnp.float32)).astype(jnp.bfloat16)
 
-    kron_high, kron_low = halves(kron[...])
+    def spread(value):
+        pick_t = lax.broadcasted_iota(jnp.int32, (TERMS * 8, TERMS), 0) >> 3
+        pick_t = pick_t == lax.broadcasted_iota(jnp.int32, (TERMS * 8, TERMS), 1)
+        pick_e = lax.broadcasted_iota(jnp.int32, (ENERGIES, ENERGIES * 8), 1) >> 3
+        pick_e = pick_e == lax.broadcasted_iota(jnp.int32, (ENERGIES, ENERGIES * 8), 0)
+        same = lax.broadcasted_iota(jnp.int32, (TERMS * 8, ENERGIES * 8), 0)
+        same = (same & 7) == (lax.broadcasted_iota(jnp.int32, (TERMS * 8, ENERGIES * 8), 1) & 7)
+        flag = lambda mask: jnp.where(mask, 1.0, 0.0).astype(jnp.bfloat16)
+        tall = jnp.dot(flag(pick_t), value, preferred_element_type=jnp.float32).astype(jnp.bfloat16)
+        wide = jnp.dot(tall, flag(pick_e), preferred_element_type=jnp.float32)
+        return jnp.where(same, wide, 0.0).astype(jnp.bfloat16)
+
+    kron_high, kron_low = [spread(part) for part in halves(coefs[...])]
 
     def weigh(c):
         for j in range(DEPTH):
@@ -305,26 +323,28 @@
                 rwin[j, 1, 4 * p + q] = unpack(4 + p, j, q)
     weigh(1)
 
-    def adjoint(i, sums_in):
-        t = TERMS - 1 - i
+    def adjoint(half, sums_in):
         grads = list(sums_in)
-        for v in range(2):
-            for j in range(DEPTH):
-                here, sums = beside(adjs, t + 1, v, j)
-                grads[j] = grads[j] + here[0] * states[t, v, j, 0]
-                for c in range(2):
-                    source = weights[j, c, t] * signs[v, j, c]
-                    adjs[t, v, j, c] = (source + onsite[j, c] * here[c]) - (twice * sums[c] + adjs[t + 2, v, j, c])
+        for step in range(2):
+            now, then = (adj_even, adj_odd) if step == 0 else (adj_odd, adj_even)
+            t = TERMS - 1 - step - 2 * half
+            for v in range(2):
+                for j in range(DEPTH):
+                    here, sums = beside(now, v, j)
+                    grads[j] = grads[j] + here[0] * states[t, v, j]
+                    for c in range(2):
+                        source = weights[j, c, t] * signs[v, j, c]
+                        then[v, j, c] = (source + onsite[j, c] * here[c]) - (twice * sums[c] + then[v, j, c])
         return tuple(grads)
 
     zero = jnp.zeros((8, LANES), jnp.float32)
-    grads = lax.fori_loop(0, TERMS, adjoint, (zero,) * DEPTH)
+    grads = lax.fori_loop(0, TERMS // 2, adjoint, (zero,) * DEPTH)
 
     for j in range(DEPTH):
         gbuf[rows(j)] = grads[j]
         for k in range(2):
             for v in range(2):
-                obuf[k, v, rows(j)] = adjs[k, v, j, 0]
+                obuf[k, v, rows(j)] = (adj_even, adj_odd)[k][v, j, 0]
     c_grad = to_x(gbuf.at[other], gother, X_GRAD)
     c_out = to_x(obuf.at[:, :, other], adj_out.at[:, mine], X_OUT)
     adj_out[:, mine] = obuf[:, :, own]
@@ -357,9 +377,6 @@
     coefficients = window_coefs(first_segment, energies)
     inv_count = 1.0 / (n_y * vector_bits.shape[0])
     scal = jnp.stack([pot_factor, twice, jnp.float32(inv_count)])
-    spread = coefficients[:, None, :, None] * jnp.eye(8, dtype=jnp.float32)[None, :, None, :]
-    spread = spread.reshape(TERMS * 8, ENERGIES * 8)
-    kron = spread
     f32, i32 = jnp.float32, jnp.int32
     vmem = pl.BlockSpec(memory_space=pltpu.VMEM)
     tile = (8, LANES)
@@ -379,8 +396,11 @@
             pltpu.VMEM((ENERGIES, 2 * ROWS, LANES), f32),
             pltpu.VMEM((2, PACKS, DEPTH) + tile, f32),
             pltpu.VMEM((2, PACKS, DEPTH) + tile, f32),
-            pltpu.VMEM((TERMS, 2, DEPTH, 2) + tile, f32),
-            pltpu.VMEM((TERMS + 2, 2, DEPTH, 2) + tile, f32),
+            pltpu.VMEM((TERMS, 2, DEPTH) + tile, f32),
+            pltpu.VMEM((2, 2, DEPTH, 2) + tile, f32),
+            pltpu.VMEM((2, 2, DEPTH, 2) + tile, f32),
+            pltpu.VMEM((2, DEPTH, 2) + tile, f32),
+            pltpu.VMEM((2, DEPTH, 2) + tile, f32),
             pltpu.VMEM((DEPTH, 2) + tile, f32),
             pltpu.VMEM((2, DEPTH, 2) + tile, f32),
             pltpu.VMEM((DEPTH, 2, ENERGIES) + tile, f32),
@@ -399,7 +419,7 @@
         compiler_params=pltpu.CompilerParams(
             collective_id=0, has_side_effects=True, vmem_limit_bytes=40 * 1024 * 1024
         ),
-    )(scal, kron, checkpoints, adjoints_in, vector_bits, potential_int, residual)
+    )(scal, coefficients, checkpoints, adjoints_in, vector_bits, potential_int, residual)
     return gradient, adjoint_out
 
 

time: 90.6 us -> 42.4 us (0.47)
  Pallas kernels: 84.8 us -> 34.3 us
  local copies, waits for them, and re-layouts: 2.4 us -> 5.36 us
    pallas_call x1, Pallas kernels: 84.8 us -> 34.3 us  [windowed(): pl.pallas_call(kernel, out_shape=(jax.ShapeDtypeStruct(potential_int.shap...]
    unnamed x12 -> x14, local copies, waits for them, and re-layouts: 1.29 us -> 5.36 us
    mul x1 -> x0, local copies, waits for them, and re-layouts: 1.04 us -> none  [windowed(): coefficients[:, None, :, None]]
where the time goes in v2:
time: 42.4 us; the launch traced here: 42.1 us
  Pallas kernels  34.3 us (81%)
  local copies, waits for them, and re-layouts  5.36 us (13%)
  between operations  2.03 us (5%)
    pallas_call x1, Pallas kernels, windowed(): pl.pallas_call(kernel, out_shape=(jax.ShapeDtypeStruct(potential_int.shap...  34.3 us
    unnamed x14, local copies, waits for them, and re-layouts  5.36 us

profile of v2, /device:TPU:0, one launch (start us, length us, event | category | flops | bytes accessed | tf_op | source)
XLA Modules:
  0.0 42.1 jit_solution(3314809404550554636)
XLA Ops:
  1.9 0.0 copy-start.5
  1.9 0.0 copy-start.4
  2.0 0.1 pad_maximum_fusion.scal
  2.1 0.5 %copy-done.5 = f32[16]{0:T(128)S(1)} copy-done((f32[16]{0:T(128)S(1)}, f32[16]{0:T(128)}, u32[]{:S(2)}) %copy-start.5) | copy-done | bytes 88
  2.6 0.1 sine_multiply_fusion
  2.7 0.1 multiply_divide_fusion.coefs
  2.8 0.0 copy-done.4
  2.8 0.0 copy-start
  2.8 0.9 %copy-done = f32[2,2,4,32,128]{4,3,2,1,0:T(8,128)S(1)} copy-done((f32[2,2,4,32,128]{4,3,2,1,0:T(8,128)S(1)}, f32[2,2,4,32,128]{4,3,2,1,0:T(8,128)}, u32[]{:S(2)}) %copy-start) | copy-done | bytes 262168
  3.8 0.0 copy-start.1
  3.8 0.9 %copy-done.1 = f32[16,32,128]{2,1,0:T(8,128)S(1)} copy-done((f32[16,32,128]{2,1,0:T(8,128)S(1)}, f32[16,32,128]{2,1,0:T(8,128)}, u32[]{:S(2)}) %copy-start.1) | copy-done | bytes 262168
  4.7 0.0 copy-start.2
  4.7 0.9 %copy-done.2 = f32[2,4,32,128]{3,2,1,0:T(8,128)S(1)} copy-done((f32[2,4,32,128]{3,2,1,0:T(8,128)S(1)}, f32[2,4,32,128]{3,2,1,0:T(8,128)}, u32[]{:S(2)}) %copy-start.2) | copy-done | bytes 131096
  5.6 0.0 copy-start.3
  5.6 0.8 %copy-done.3 = s32[4,32,128]{2,1,0:T(8,128)S(1)} copy-done((s32[4,32,128]{2,1,0:T(8,128)S(1)}, s32[4,32,128]{2,1,0:T(8,128)}, u32[]{:S(2)}) %copy-start.3) | copy-done | bytes 65560
  6.5 34.3 %shard_map.95 = (f32[32,128]{1,0:T(8,128)S(1)}, f32[2,4,32,128]{3,2,1,0:T(8,128)S(1)}) custom-call(f32[3]{0:T(128)S(1)} %pad_maximum_fusion.scal, f32[32,16]{1,0:T(8,128)S(1)} %multiply_divide_fusion.coefs, f32[2,2,4,32,128]{4,3,2,1,0:T(8,128)S(1)} %copy-done, f32[2,4,32,128]{3,2,1,0:T(8,128)S(1)} %copy-done.2, s32[4,32,128]{2,1,0:T(8,128)S(1)} %copy-done.3, ...), custom_call_target="tpu_custom_call" | custom-call | tf_op jit(solution)/shard_map/pallas_call | solution.py:383
  40.8 0.6 %copy.15 = f32[32,128]{1,0:T(8,128)} copy(f32[32,128]{1,0:T(8,128)S(1)} %get-tuple-element.6) | data formatting | bytes 32768
  41.4 0.7 %copy.16 = f32[2,4,32,128]{3,2,1,0:T(8,128)} copy(f32[2,4,32,128]{3,2,1,0:T(8,128)S(1)} %get-tuple-element.7) | data formatting | bytes 262144
  (2 shorter events, 0.1 us)
Async XLA Ops:
  1.9 0.7 %copy-start.5 = (f32[16]{0:T(128)S(1)}, f32[16]{0:T(128)}, u32[]{:S(2)}) copy-start(f32[16]{0:T(128)} %param.13) | copy-start | bytes 196
  1.9 0.9 %copy-start.4 = (s32[32,128]{1,0:T(8,128)S(1)}, s32[32,128]{1,0:T(8,128)}, u32[]{:S(2)}) copy-start(s32[32,128]{1,0:T(8,128)} %pot.1) | copy-start | bytes 49156
  2.8 1.0 %copy-start = (f32[2,2,4,32,128]{4,3,2,1,0:T(8,128)S(1)}, f32[2,2,4,32,128]{4,3,2,1,0:T(8,128)}, u32[]{:S(2)}) copy-start(f32[2,2,4,32,128]{4,3,2,1,0:T(8,128)} %ck.1) | copy-start | bytes 786436
  3.8 0.9 %copy-start.1 = (f32[16,32,128]{2,1,0:T(8,128)S(1)}, f32[16,32,128]{2,1,0:T(8,128)}, u32[]{:S(2)}) copy-start(f32[16,32,128]{2,1,0:T(8,128)} %res.1) | copy-start | bytes 786436
  4.7 0.9 %copy-start.2 = (f32[2,4,32,128]{3,2,1,0:T(8,128)S(1)}, f32[2,4,32,128]{3,2,1,0:T(8,128)}, u32[]{:S(2)}) copy-start(f32[2,4,32,128]{3,2,1,0:T(8,128)} %adj.1) | copy-start | bytes 393220
  5.6 0.8 %copy-start.3 = (s32[4,32,128]{2,1,0:T(8,128)S(1)}, s32[4,32,128]{2,1,0:T(8,128)}, u32[]{:S(2)}) copy-start(s32[4,32,128]{2,1,0:T(8,128)} %bits.1) | copy-start | bytes 196612

commit v3 on v2

--- a/solution.py
+++ b/solution.py
@@ -112,14 +112,16 @@
 ENERGIES = 16
 X_CK, X_ADJ, X_BITS, X_POT, X_RES, X_GRAD, X_OUT = range(7)
 Z_CK, Z_ADJ, Z_RES = range(3)
-Z_PARTS = ((0, 2), (2, 2), (4, 4))
-PACKS = 8
-
-
-def pick_quarter(lane, parts):
-    low = jnp.where(lane < REACH, parts[0], parts[1])
-    high = jnp.where(lane < 3 * REACH, parts[2], parts[3])
-    return jnp.where(lane < 2 * REACH, low, high)
+V_ROWS, V_HALO, V_GRAD = range(3)
+QUARTER = 4
+
+
+def pick(lane, parts):
+    width = LANES // len(parts)
+    while len(parts) > 1:
+        parts = [jnp.where((lane & width) == 0, low, high) for low, high in zip(parts[::2], parts[1::2])]
+        width = 2 * width
+    return parts[0]
 
 
 def turn(value, shift):
@@ -129,7 +131,7 @@
 
 def kernel(
     scal, coefs, ck, adj, bits, pot, res, grad_out, adj_out,
-    wck, wadj, wbits, wpot, wres, zsend, zrecv, states, even, odd, adj_even, adj_odd, onsite, signs, rwin, weights,
+    wck, wadj, wbits, wpot, wres, zsend, zrecv, zres, states, even, odd, adj_even, adj_odd, onsite, signs, rwin, weights,
     gbuf, gother, gall, obuf, xs, xr, zs, zr, vs, vr,
 ):
     x = lax.axis_index("row")
@@ -162,11 +164,12 @@
     mine = pl.ds(2 * x, 2)
     other = pl.ds(ROWS, ROWS)
     own = pl.ds(0, ROWS)
+    share = pl.ds(QUARTER * y, QUARTER)
+    c_res = to_x(res.at[share], wres.at[share, other], X_RES)
     c_ck = to_x(ck.at[:, :, theirs], wck.at[:, :, :, other], X_CK)
     c_adj = to_x(adj.at[:, theirs], wadj.at[:, :, other], X_ADJ)
     c_bits = to_x(bits.at[theirs], wbits.at[:, other], X_BITS)
     c_pot = to_x(pot, wpot.at[other], X_POT)
-    c_res = to_x(res, wres.at[:, other], X_RES)
 
     wck[:, :, :, own] = ck[:, :, mine]
     wadj[:, :, own] = adj[:, mine]
@@ -180,31 +183,46 @@
         return pl.ds(j, 8, stride=8)
 
     def pack(slot, j, planes):
-        zsend[0, slot, j] = pick_quarter(lane, [turn(p, REACH * (q + 1)) for q, p in enumerate(planes)])
-        zsend[1, slot, j] = pick_quarter(lane, [turn(p, REACH * q) for q, p in enumerate(planes)])
-
-    def unpack(slot, j, q):
-        from_left = turn(zrecv[0, slot, j], LANES - REACH - REACH * q)
-        from_right = turn(zrecv[1, slot, j], LANES - REACH * q)
-        return jnp.where(lane < 2 * REACH, from_right, from_left)
-
-    def to_z(part):
-        first, count = Z_PARTS[part]
-        span = pl.ds(first, count)
+        width = LANES // len(planes)
+        zsend[0, slot, j] = pick(lane, [turn(p, width * (q + 1)) for q, p in enumerate(planes)])
+        zsend[1, slot, j] = pick(lane, [turn(p, width * q) for q, p in enumerate(planes)])
+
+    def unpack(pair, q, count):
+        width = LANES // count
+        from_left = turn(pair[0], LANES - width - width * q)
+        from_right = turn(pair[1], LANES - width * q)
+        return jnp.where(lane < LANES // 2, from_right, from_left)
+
+    def to_z(part, source, target):
         return [
-            remote(zsend.at[d, span], zrecv.at[d, span], zs.at[d, part], zr.at[d, part], device)
+            remote(source.at[d], target.at[d], zs.at[d, part], zr.at[d, part], device)
             for d, device in enumerate((right, left))
         ]
 
+    def to_peers(part, ref):
+        return [
+            remote(ref, ref, vs.at[part, d], vr.at[part, d], device) for d, device in enumerate(peers)
+        ]
+
+    def settle(copies):
+        for copy in copies:
+            copy.wait()
+
+    c_res.wait()
+    g_rows = to_peers(V_ROWS, wres.at[share, other])
+    for j in range(DEPTH):
+        pack(3, j, [wres[QUARTER * y + q, rows(j)] for q in range(QUARTER)])
+    z_res = to_z(Z_RES, zsend.at[:, 3], zres.at[:, y])
+
     c_ck.wait()
     for j in range(DEPTH):
-        for s in range(2):
-            planes = [wck[s, k, v, rows(j)] for k in range(2) for v in range(2)]
-            pack(s, j, planes)
-            for q, plane in enumerate(planes):
-                states[s * SEG + q // 2, q % 2, j] = plane
-                (even, odd)[q // 2][s, q % 2, j, 0] = plane
-    z_ck = to_z(Z_CK)
+        planes = [wck[s, k, v, rows(j)] for s in range(2) for k in range(2) for v in range(2)]
+        pack(0, j, planes)
+        for q, plane in enumerate(planes):
+            s, k, v = q // 4, q // 2 % 2, q % 2
+            states[s * SEG + k, v, j] = plane
+            (even, odd)[k][s, v, j, 0] = plane
+    z_ck = to_z(Z_CK, zsend.at[:, pl.ds(0, 1)], zrecv.at[:, pl.ds(0, 1)])
 
     pot_factor = scal[0]
     twice = scal[1]
@@ -214,42 +232,70 @@
     c_pot.wait()
     for j in range(DEPTH):
         planes = [wadj[k, v, rows(j)] for k in range(2) for v in range(2)]
-        pack(2, j, planes)
+        pack(1, j, planes)
         for q, plane in enumerate(planes):
             (adj_even, adj_odd)[q // 2][q % 2, j, 0] = plane
         sign = [(2 * wbits[v, rows(j)] - 1).astype(jnp.float32) * inv_count for v in range(2)]
         site = wpot[rows(j)].astype(jnp.float32) * pot_factor * twice
-        pack(3, j, [sign[0], sign[1], site, site])
+        pack(2, j, [sign[0], sign[1], site, site])
         signs[0, j, 0] = sign[0]
         signs[1, j, 0] = sign[1]
         onsite[j, 0] = site
-    z_adj = to_z(Z_ADJ)
-
-    c_res.wait()
-    for j in range(DEPTH):
-        for p in range(4):
-            planes = [wres[4 * p + q, rows(j)] for q in range(4)]
-            pack(4 + p, j, planes)
-            for q, plane in enumerate(planes):
-                rwin[j, 0, 4 * p + q] = plane
-    z_res = to_z(Z_RES)
-
-    def settle(copies):
-        for copy in copies:
-            copy.wait()
+    z_adj = to_z(Z_ADJ, zsend.at[:, pl.ds(1, 2)], zrecv.at[:, pl.ds(1, 2)])
+
+    settle(z_res)
+    g_halo = to_peers(V_HALO, zres.at[:, y])
+
+    def halves(value):
+        high = value.astype(jnp.bfloat16)
+        return high, (value - high.astype(jnp.float32)).astype(jnp.bfloat16)
+
+    def spread(value):
+        pick_t = lax.broadcasted_iota(jnp.int32, (TERMS * 8, TERMS), 0) >> 3
+        pick_t = pick_t == lax.broadcasted_iota(jnp.int32, (TERMS * 8, TERMS), 1)
+        pick_e = lax.broadcasted_iota(jnp.int32, (ENERGIES, ENERGIES * 8), 1) >> 3
+        pick_e = pick_e == lax.broadcasted_iota(jnp.int32, (ENERGIES, ENERGIES * 8), 0)
+        same = lax.broadcasted_iota(jnp.int32, (TERMS * 8, ENERGIES * 8), 0)
+        same = (same & 7) == (lax.broadcasted_iota(jnp.int32, (TERMS * 8, ENERGIES * 8), 1) & 7)
+        flag = lambda mask: jnp.where(mask, 1.0, 0.0).astype(jnp.bfloat16)
+        tall = jnp.dot(flag(pick_t), value, preferred_element_type=jnp.float32).astype(jnp.bfloat16)
+        wide = jnp.dot(tall, flag(pick_e), preferred_element_type=jnp.float32)
+        return jnp.where(same, wide, 0.0).astype(jnp.bfloat16)
+
+    kron_high, kron_low = [spread(part) for part in halves(coefs[...])]
+
+    kron_wide = jnp.concatenate([kron_high, kron_high], axis=1)
+
+    def weigh(c):
+        for j in range(0, DEPTH, 2):
+            block = [rwin[j + i, c].reshape(ENERGIES * 8, LANES) for i in range(2)]
+            high, low = halves(jnp.concatenate(block, axis=1))
+            total = jnp.dot(kron_wide, jnp.concatenate([high, low], axis=0), preferred_element_type=jnp.float32)
+            total = total + jnp.dot(kron_low, high, preferred_element_type=jnp.float32)
+            for i in range(2):
+                weights[j + i, c] = total[:, i * LANES : (i + 1) * LANES].reshape(TERMS, 8, LANES)
+
+    settle(g_rows)
+    for j in range(DEPTH):
+        for e in range(ENERGIES):
+            rwin[j, 0, e] = wres[e, rows(j)]
+    weigh(0)
 
     settle(z_ck)
     for j in range(DEPTH):
-        for s in range(2):
-            for q in range(4):
-                (even, odd)[q // 2][s, q % 2, j, 1] = unpack(s, j, q)
+        pair = [zrecv[d, 0, j] for d in range(2)]
+        for q in range(8):
+            s, k, v = q // 4, q // 2 % 2, q % 2
+            (even, odd)[k][s, v, j, 1] = unpack(pair, q, 8)
     settle(z_adj)
     for j in range(DEPTH):
+        pair = [zrecv[d, 1, j] for d in range(2)]
         for q in range(4):
-            (adj_even, adj_odd)[q // 2][q % 2, j, 1] = unpack(2, j, q)
-        signs[0, j, 1] = unpack(3, j, 0)
-        signs[1, j, 1] = unpack(3, j, 1)
-        onsite[j, 1] = unpack(3, j, 2)
+            (adj_even, adj_odd)[q // 2][q % 2, j, 1] = unpack(pair, q, 4)
+        pair = [zrecv[d, 2, j] for d in range(2)]
+        signs[0, j, 1] = unpack(pair, 0, 4)
+        signs[1, j, 1] = unpack(pair, 1, 4)
+        onsite[j, 1] = unpack(pair, 2, 4)
 
     first_lane = lane == 0
     last_lane = lane == LANES - 1
@@ -290,37 +336,11 @@
 
     lax.fori_loop(0, SEG // 2 - 1, forward, 0)
 
-    def halves(value):
-        high = value.astype(jnp.bfloat16)
-        return high, (value - high.astype(jnp.float32)).astype(jnp.bfloat16)
-
-    def spread(value):
-        pick_t = lax.broadcasted_iota(jnp.int32, (TERMS * 8, TERMS), 0) >> 3
-        pick_t = pick_t == lax.broadcasted_iota(jnp.int32, (TERMS * 8, TERMS), 1)
-        pick_e = lax.broadcasted_iota(jnp.int32, (ENERGIES, ENERGIES * 8), 1) >> 3
-        pick_e = pick_e == lax.broadcasted_iota(jnp.int32, (ENERGIES, ENERGIES * 8), 0)
-        same = lax.broadcasted_iota(jnp.int32, (TERMS * 8, ENERGIES * 8), 0)
-        same = (same & 7) == (lax.broadcasted_iota(jnp.int32, (TERMS * 8, ENERGIES * 8), 1) & 7)
-        flag = lambda mask: jnp.where(mask, 1.0, 0.0).astype(jnp.bfloat16)
-        tall = jnp.dot(flag(pick_t), value, preferred_element_type=jnp.float32).astype(jnp.bfloat16)
-        wide = jnp.dot(tall, flag(pick_e), preferred_element_type=jnp.float32)
-        return jnp.where(same, wide, 0.0).astype(jnp.bfloat16)
-
-    kron_high, kron_low = [spread(part) for part in halves(coefs[...])]
-
-    def weigh(c):
-        for j in range(DEPTH):
-            high, low = halves(rwin[j, c].reshape(ENERGIES * 8, LANES))
-            dot = lambda a, b: jnp.dot(a, b, preferred_element_type=jnp.float32)
-            total = dot(kron_high, high) + (dot(kron_high, low) + dot(kron_low, high))
-            weights[j, c] = total.reshape(TERMS, 8, LANES)
-
-    weigh(0)
-    settle(z_res)
-    for j in range(DEPTH):
-        for p in range(4):
-            for q in range(4):
-                rwin[j, 1, 4 * p + q] = unpack(4 + p, j, q)
+    settle(g_halo)
+    for j in range(DEPTH):
+        for e in range(ENERGIES):
+            pair = [zres[d, e // QUARTER, j] for d in range(2)]
+            rwin[j, 1, e] = unpack(pair, e % QUARTER, QUARTER)
     weigh(1)
 
     def adjoint(half, sums_in):
@@ -350,10 +370,7 @@
     adj_out[:, mine] = obuf[:, :, own]
     c_grad.wait()
     gall[y] = gbuf[own] + gother[...]
-    shares = [
-        remote(gall.at[y], gall.at[y], vs.at[d], vr.at[d], device) for d, device in enumerate(peers)
-    ]
-    settle(shares)
+    settle(to_peers(V_GRAD, gall.at[y]))
     total = gall[0]
     for d in range(1, n_y):
         total = total + gall[d]
@@ -394,8 +411,9 @@
             pltpu.VMEM((2, 2 * ROWS, LANES), i32),
             pltpu.VMEM((2 * ROWS, LANES), i32),
             pltpu.VMEM((ENERGIES, 2 * ROWS, LANES), f32),
-            pltpu.VMEM((2, PACKS, DEPTH) + tile, f32),
-            pltpu.VMEM((2, PACKS, DEPTH) + tile, f32),
+            pltpu.VMEM((2, 4, DEPTH) + tile, f32),
+            pltpu.VMEM((2, 3, DEPTH) + tile, f32),
+            pltpu.VMEM((2, n_y, DEPTH) + tile, f32),
             pltpu.VMEM((TERMS, 2, DEPTH) + tile, f32),
             pltpu.VMEM((2, 2, DEPTH, 2) + tile, f32),
             pltpu.VMEM((2, 2, DEPTH, 2) + tile, f32),
@@ -413,8 +431,8 @@
             pltpu.SemaphoreType.DMA((7,)),
             pltpu.SemaphoreType.DMA((2, 3)),
             pltpu.SemaphoreType.DMA((2, 3)),
-            pltpu.SemaphoreType.DMA((n_y - 1,)),
-            pltpu.SemaphoreType.DMA((n_y - 1,)),
+            pltpu.SemaphoreType.DMA((3, n_y - 1)),
+            pltpu.SemaphoreType.DMA((3, n_y - 1)),
         ],
         compiler_params=pltpu.CompilerParams(
             collective_id=0, has_side_effects=True, vmem_limit_bytes=40 * 1024 * 1024
@@ -424,7 +442,7 @@
 
 
 def solution(mesh):
-    fits = mesh.shape["row"] == 2 and mesh.shape["col"] > 2
+    fits = mesh.shape["row"] == 2 and mesh.shape["col"] > 2 and mesh.shape["vec"] == 4
     return jax.shard_map(
         windowed if fits else per_device,
         mesh=mesh,

time: 42.4 us -> 39.2 us (0.925)
  Pallas kernels: 34.3 us -> 31.2 us
    pallas_call x1, Pallas kernels: 34.3 us -> 31.2 us  [windowed(): pl.pallas_call(kernel, out_shape=(jax.ShapeDtypeStruct(potential_int.shap...]
where the time goes in v3:
time: 39.2 us; the launch traced here: 38.9 us
  Pallas kernels  31.2 us (80%)
  local copies, waits for them, and re-layouts  5.36 us (14%)
  between operations  2.03 us (5%)
    pallas_call x1, Pallas kernels, windowed(): pl.pallas_call(kernel, out_shape=(jax.ShapeDtypeStruct(potential_int.shap...  31.2 us
    unnamed x14, local copies, waits for them, and re-layouts  5.36 us

profile of v3, /device:TPU:0, one launch (start us, length us, event | category | flops | bytes accessed | tf_op | source)
XLA Modules:
  0.0 38.9 jit_solution(3539045810418933457)
XLA Ops:
  1.9 0.0 copy-start.5
  1.9 0.0 copy-start.4
  2.0 0.1 pad_maximum_fusion.scal
  2.1 0.5 %copy-done.5 = f32[16]{0:T(128)S(1)} copy-done((f32[16]{0:T(128)S(1)}, f32[16]{0:T(128)}, u32[]{:S(2)}) %copy-start.5) | copy-done | bytes 88
  2.6 0.1 sine_multiply_fusion
  2.7 0.1 multiply_divide_fusion.coefs
  2.8 0.0 copy-done.4
  2.8 0.0 copy-start
  2.8 0.9 %copy-done = f32[2,2,4,32,128]{4,3,2,1,0:T(8,128)S(1)} copy-done((f32[2,2,4,32,128]{4,3,2,1,0:T(8,128)S(1)}, f32[2,2,4,32,128]{4,3,2,1,0:T(8,128)}, u32[]{:S(2)}) %copy-start) | copy-done | bytes 262168
  3.8 0.0 copy-start.1
  3.8 0.9 %copy-done.1 = f32[16,32,128]{2,1,0:T(8,128)S(1)} copy-done((f32[16,32,128]{2,1,0:T(8,128)S(1)}, f32[16,32,128]{2,1,0:T(8,128)}, u32[]{:S(2)}) %copy-start.1) | copy-done | bytes 262168
  4.7 0.0 copy-start.2
  4.7 0.9 %copy-done.2 = f32[2,4,32,128]{3,2,1,0:T(8,128)S(1)} copy-done((f32[2,4,32,128]{3,2,1,0:T(8,128)S(1)}, f32[2,4,32,128]{3,2,1,0:T(8,128)}, u32[]{:S(2)}) %copy-start.2) | copy-done | bytes 131096
  5.6 0.0 copy-start.3
  5.6 0.8 %copy-done.3 = s32[4,32,128]{2,1,0:T(8,128)S(1)} copy-done((s32[4,32,128]{2,1,0:T(8,128)S(1)}, s32[4,32,128]{2,1,0:T(8,128)}, u32[]{:S(2)}) %copy-start.3) | copy-done | bytes 65560
  6.5 31.2 %shard_map.95 = (f32[32,128]{1,0:T(8,128)S(1)}, f32[2,4,32,128]{3,2,1,0:T(8,128)S(1)}) custom-call(f32[3]{0:T(128)S(1)} %pad_maximum_fusion.scal, f32[32,16]{1,0:T(8,128)S(1)} %multiply_divide_fusion.coefs, f32[2,2,4,32,128]{4,3,2,1,0:T(8,128)S(1)} %copy-done, f32[2,4,32,128]{3,2,1,0:T(8,128)S(1)} %copy-done.2, s32[4,32,128]{2,1,0:T(8,128)S(1)} %copy-done.3, ...), custom_call_target="tpu_custom_call" | custom-call | tf_op jit(solution)/shard_map/pallas_call | solution.py:400
  37.7 0.6 %copy.15 = f32[32,128]{1,0:T(8,128)} copy(f32[32,128]{1,0:T(8,128)S(1)} %get-tuple-element.6) | data formatting | bytes 32768
  38.3 0.7 %copy.16 = f32[2,4,32,128]{3,2,1,0:T(8,128)} copy(f32[2,4,32,128]{3,2,1,0:T(8,128)S(1)} %get-tuple-element.7) | data formatting | bytes 262144
  (2 shorter events, 0.1 us)
Async XLA Ops:
  1.9 0.7 %copy-start.5 = (f32[16]{0:T(128)S(1)}, f32[16]{0:T(128)}, u32[]{:S(2)}) copy-start(f32[16]{0:T(128)} %param.13) | copy-start | bytes 196
  1.9 0.9 %copy-start.4 = (s32[32,128]{1,0:T(8,128)S(1)}, s32[32,128]{1,0:T(8,128)}, u32[]{:S(2)}) copy-start(s32[32,128]{1,0:T(8,128)} %pot.1) | copy-start | bytes 49156
  2.8 1.0 %copy-start = (f32[2,2,4,32,128]{4,3,2,1,0:T(8,128)S(1)}, f32[2,2,4,32,128]{4,3,2,1,0:T(8,128)}, u32[]{:S(2)}) copy-start(f32[2,2,4,32,128]{4,3,2,1,0:T(8,128)} %ck.1) | copy-start | bytes 786436
  3.8 0.9 %copy-start.1 = (f32[16,32,128]{2,1,0:T(8,128)S(1)}, f32[16,32,128]{2,1,0:T(8,128)}, u32[]{:S(2)}) copy-start(f32[16,32,128]{2,1,0:T(8,128)} %res.1) | copy-start | bytes 786436
  4.7 0.9 %copy-start.2 = (f32[2,4,32,128]{3,2,1,0:T(8,128)S(1)}, f32[2,4,32,128]{3,2,1,0:T(8,128)}, u32[]{:S(2)}) copy-start(f32[2,4,32,128]{3,2,1,0:T(8,128)} %adj.1) | copy-start | bytes 393220
  5.6 0.8 %copy-start.3 = (s32[4,32,128]{2,1,0:T(8,128)S(1)}, s32[4,32,128]{2,1,0:T(8,128)}, u32[]{:S(2)}) copy-start(s32[4,32,128]{2,1,0:T(8,128)} %bits.1) | copy-start | bytes 196612

commit v4 on v3

--- a/solution.py
+++ b/solution.py
@@ -110,9 +110,9 @@
 REACH = 32
 DEPTH = 8
 ENERGIES = 16
-X_CK, X_ADJ, X_BITS, X_POT, X_RES, X_GRAD, X_OUT = range(7)
+X_CK, X_ADJ, X_BITS, X_POT, X_RES, X_OUT = range(6)
 Z_CK, Z_ADJ, Z_RES = range(3)
-V_ROWS, V_HALO, V_GRAD = range(3)
+V_ROWS, V_HALO, V_GRAD, V_CROSS = range(4)
 QUARTER = 4
 
 
@@ -132,7 +132,7 @@
 def kernel(
     scal, coefs, ck, adj, bits, pot, res, grad_out, adj_out,
     wck, wadj, wbits, wpot, wres, zsend, zrecv, zres, states, even, odd, adj_even, adj_odd, onsite, signs, rwin, weights,
-    gbuf, gother, gall, obuf, xs, xr, zs, zr, vs, vr,
+    gbuf, gall, obuf, ls, xs, xr, zs, zr, vs, vr,
 ):
     x = lax.axis_index("row")
     z = lax.axis_index("col")
@@ -143,11 +143,12 @@
     right = {"col": lax.rem(z + 1, n_z)}
     left = {"col": lax.rem(z + n_z - 1, n_z)}
     peers = [{"vec": lax.rem(y + d, n_y)} for d in range(1, n_y)]
+    far = [{"row": 1 - x, "vec": lax.rem(y + d, n_y)} for d in range(n_y)]
 
     barrier = pltpu.get_barrier_semaphore()
-    for device in [across, right, left] + peers:
+    for device in [right, left] + peers + far:
         pl.semaphore_signal(barrier, inc=1, device_id=device, device_id_type=MESH)
-    pl.semaphore_wait(barrier, 3 + len(peers))
+    pl.semaphore_wait(barrier, 2 + len(peers) + len(far))
 
     def remote(source, target, send, recv, device):
         copy = pltpu.make_async_remote_copy(
@@ -171,11 +172,16 @@
     c_bits = to_x(bits.at[theirs], wbits.at[:, other], X_BITS)
     c_pot = to_x(pot, wpot.at[other], X_POT)
 
-    wck[:, :, :, own] = ck[:, :, mine]
-    wadj[:, :, own] = adj[:, mine]
-    wbits[:, own] = bits[mine]
-    wpot[own] = pot[...]
-    wres[:, own] = res[...]
+    def local(source, target, index):
+        copy = pltpu.make_async_copy(source, target, ls.at[index])
+        copy.start()
+        return copy
+
+    l_res = local(res, wres.at[:, own], X_RES)
+    l_ck = local(ck.at[:, :, mine], wck.at[:, :, :, own], X_CK)
+    l_adj = local(adj.at[:, mine], wadj.at[:, :, own], X_ADJ)
+    l_bits = local(bits.at[mine], wbits.at[:, own], X_BITS)
+    l_pot = local(pot, wpot.at[own], X_POT)
 
     lane = lax.broadcasted_iota(jnp.int32, (8, LANES), 1)
 
@@ -199,21 +205,26 @@
             for d, device in enumerate((right, left))
         ]
 
+    def fan(part, source, target, devices):
+        return [
+            remote(source, target, vs.at[part, d], vr.at[part, d], device) for d, device in enumerate(devices)
+        ]
+
     def to_peers(part, ref):
-        return [
-            remote(ref, ref, vs.at[part, d], vr.at[part, d], device) for d, device in enumerate(peers)
-        ]
+        return fan(part, ref, ref, peers)
 
     def settle(copies):
         for copy in copies:
             copy.wait()
 
+    l_res.wait()
     c_res.wait()
     g_rows = to_peers(V_ROWS, wres.at[share, other])
     for j in range(DEPTH):
         pack(3, j, [wres[QUARTER * y + q, rows(j)] for q in range(QUARTER)])
     z_res = to_z(Z_RES, zsend.at[:, 3], zres.at[:, y])
 
+    l_ck.wait()
     c_ck.wait()
     for j in range(DEPTH):
         planes = [wck[s, k, v, rows(j)] for s in range(2) for k in range(2) for v in range(2)]
@@ -227,6 +238,7 @@
     pot_factor = scal[0]
     twice = scal[1]
     inv_count = scal[2]
+    settle([l_adj, l_bits, l_pot])
     c_adj.wait()
     c_bits.wait()
     c_pot.wait()
@@ -365,17 +377,20 @@
         for k in range(2):
             for v in range(2):
                 obuf[k, v, rows(j)] = (adj_even, adj_odd)[k][v, j, 0]
-    c_grad = to_x(gbuf.at[other], gother, X_GRAD)
+    sums = fan(V_CROSS, gbuf.at[other], gall.at[x, y], far)
+    gall[x, y] = gbuf[own]
+    sums += to_peers(V_GRAD, gall.at[x, y])
     c_out = to_x(obuf.at[:, :, other], adj_out.at[:, mine], X_OUT)
-    adj_out[:, mine] = obuf[:, :, own]
-    c_grad.wait()
-    gall[y] = gbuf[own] + gother[...]
-    settle(to_peers(V_GRAD, gall.at[y]))
-    total = gall[0]
+    l_out = local(obuf.at[:, :, own], adj_out.at[:, mine], X_OUT)
+    settle(sums)
+    total = gall[0, 0] + gall[1, 0]
     for d in range(1, n_y):
-        total = total + gall[d]
-    grad_out[...] = total * twice
+        total = total + (gall[0, d] + gall[1, d])
+    gbuf[own] = total * twice
+    l_grad = local(gbuf.at[own], grad_out, X_CK)
+    l_out.wait()
     c_out.wait()
+    l_grad.wait()
 
 
 def windowed(
@@ -403,8 +418,8 @@
             jax.ShapeDtypeStruct(potential_int.shape, f32),
             jax.ShapeDtypeStruct(adjoints_in.shape, f32),
         ),
-        in_specs=[pl.BlockSpec(memory_space=pltpu.SMEM)] + [vmem] * 6,
-        out_specs=(vmem, vmem),
+        in_specs=[pl.BlockSpec(memory_space=pltpu.SMEM), vmem] + [pl.BlockSpec(memory_space=pl.ANY)] * 5,
+        out_specs=(pl.BlockSpec(memory_space=pl.ANY),) * 2,
         scratch_shapes=[
             pltpu.VMEM((2, 2, 2, 2 * ROWS, LANES), f32),
             pltpu.VMEM((2, 2, 2 * ROWS, LANES), f32),
@@ -424,18 +439,18 @@
             pltpu.VMEM((DEPTH, 2, ENERGIES) + tile, f32),
             pltpu.VMEM((DEPTH, 2, TERMS) + tile, f32),
             pltpu.VMEM((2 * ROWS, LANES), f32),
-            pltpu.VMEM((ROWS, LANES), f32),
-            pltpu.VMEM((n_y, ROWS, LANES), f32),
+            pltpu.VMEM((2, n_y, ROWS, LANES), f32),
             pltpu.VMEM((2, 2, 2 * ROWS, LANES), f32),
-            pltpu.SemaphoreType.DMA((7,)),
-            pltpu.SemaphoreType.DMA((7,)),
+            pltpu.SemaphoreType.DMA((6,)),
+            pltpu.SemaphoreType.DMA((6,)),
+            pltpu.SemaphoreType.DMA((6,)),
             pltpu.SemaphoreType.DMA((2, 3)),
             pltpu.SemaphoreType.DMA((2, 3)),
-            pltpu.SemaphoreType.DMA((3, n_y - 1)),
-            pltpu.SemaphoreType.DMA((3, n_y - 1)),
+            pltpu.SemaphoreType.DMA((4, n_y)),
+            pltpu.SemaphoreType.DMA((4, n_y)),
         ],
         compiler_params=pltpu.CompilerParams(
-            collective_id=0, has_side_effects=True, vmem_limit_bytes=40 * 1024 * 1024
+            collective_id=0, has_side_effects=True, vmem_limit_bytes=56 * 1024 * 1024
         ),
     )(scal, coefficients, checkpoints, adjoints_in, vector_bits, potential_int, residual)
     return gradient, adjoint_out

time: 39.2 us -> 38.8 us (0.990)
  local copies, waits for them, and re-layouts: 5.36 us -> 3.53 us
  other arithmetic: 0.35 us -> 1.47 us
    unnamed x14 -> x4, local copies, waits for them, and re-layouts: 5.36 us -> 3.53 us
    div x1, other arithmetic: 0.14 us -> 0.75 us  [window_coefs(): (jackson * factor)[:, None] * cosines / (math.pi * jnp.sin(angles))[None, :]]
    another operation x1, other arithmetic: 0.08 us -> 0.59 us  [windowed(): scal = jnp.stack([pot_factor, twice, jnp.float32(inv_count)])]
where the time goes in v4:
time: 38.8 us; the launch traced here: 38.4 us
  Pallas kernels  31.4 us (81%)
  local copies, waits for them, and re-layouts  3.53 us (9%)
  between operations  2 us (5%)
  other arithmetic  1.47 us (4%)
    pallas_call x1, Pallas kernels, windowed(): pl.pallas_call(kernel, out_shape=(jax.ShapeDtypeStruct(potential_int.shap...  31.4 us
    unnamed x4, local copies, waits for them, and re-layouts  3.53 us

profile of v4, /device:TPU:0, one launch (start us, length us, event | category | flops | bytes accessed | tf_op | source)
XLA Modules:
  0.0 38.4 jit_solution(3075874058741988433)
XLA Ops:
  2.0 0.6 %pad_maximum_fusion.scal = f32[3]{0:T(128)} fusion(f32[1]{0:T(128)} %constant.8.clone.1, f32[1]{0:T(128)S(6)} %div.15, f32[1]{0:T(128)S(6)} %copy.13), kind=kLoop, calls=%fused_computation.3 | loop fusion | flops 6 | bytes 24 | tf_op jit(solution)/shard_map/stack | solution.py:411
  2.6 0.0 copy-start
  2.6 0.6 %copy-done = f32[16]{0:T(128)S(1)} copy-done((f32[16]{0:T(128)S(1)}, f32[16]{0:T(128)}, u32[]{:S(2)}) %copy-start) | copy-done | bytes 88
  3.3 0.1 sine_multiply_fusion
  3.3 0.8 %multiply_divide_fusion.coefs = f32[32,16]{1,0:T(8,128)} fusion(f32[32]{0:T(128)S(1)} %fusion, f32[16]{0:T(128)S(1)} %get-tuple-element.2, f32[16]{0:T(128)S(1)} %get-tuple-element.3, f32[32]{0:T(128)S(1)} %fusion.1), kind=kLoop, calls=%fused_computation | loop fusion | flops 1536 | bytes 2432 | tf_op jit(solution)/shard_map/div | solution.py:40
  4.1 31.4 %shard_map.95 = (f32[32,128]{1,0:T(8,128)}, f32[2,4,32,128]{3,2,1,0:T(8,128)}) custom-call(f32[3]{0:T(128)} %pad_maximum_fusion.scal, f32[32,16]{1,0:T(8,128)} %multiply_divide_fusion.coefs, f32[2,2,4,32,128]{4,3,2,1,0:T(8,128)} %ck.1, f32[2,4,32,128]{3,2,1,0:T(8,128)} %adj.1, s32[4,32,128]{2,1,0:T(8,128)} %bits.1, s32[32,128]{1,0:T(8,128)} %pot.1, ...), custom_call_target="tpu_custom_call" | custom-call | tf_op jit(solution)/shard_map/pallas_call | solution.py:415
  35.5 1.3 %copy.15 = f32[32,128]{1,0:T(8,128)} copy(f32[32,128]{1,0:T(8,128)} %get-tuple-element.6) | data formatting | bytes 32768
  36.8 1.6 %copy.16 = f32[2,4,32,128]{3,2,1,0:T(8,128)} copy(f32[2,4,32,128]{3,2,1,0:T(8,128)} %get-tuple-element.7) | data formatting | bytes 262144
  (2 shorter events, 0.1 us)
Async XLA Ops:
  2.6 0.7 %copy-start = (f32[16]{0:T(128)S(1)}, f32[16]{0:T(128)}, u32[]{:S(2)}) copy-start(f32[16]{0:T(128)} %param.13) | copy-start | bytes 196

commit v5 on v4

--- a/solution.py
+++ b/solution.py
@@ -110,7 +110,7 @@
 REACH = 32
 DEPTH = 8
 ENERGIES = 16
-X_CK, X_ADJ, X_BITS, X_POT, X_RES, X_OUT = range(6)
+X_CK, X_ADJ, X_BITS, X_POT, X_RES, X_OUT, H_CK, H_ADJ, H_BITS = range(9)
 Z_CK, Z_ADJ, Z_RES = range(3)
 V_ROWS, V_HALO, V_GRAD, V_CROSS = range(4)
 QUARTER = 4
@@ -131,7 +131,7 @@
 
 def kernel(
     scal, coefs, ck, adj, bits, pot, res, grad_out, adj_out,
-    wck, wadj, wbits, wpot, wres, zsend, zrecv, zres, states, even, odd, adj_even, adj_odd, onsite, signs, rwin, weights,
+    hck, hadj, hbits, wck, wadj, wbits, wpot, wres, zsend, zrecv, zres, states, even, odd, adj_even, adj_odd, onsite, signs, rwin, weights,
     gbuf, gall, obuf, ls, xs, xr, zs, zr, vs, vr,
 ):
     x = lax.axis_index("row")
@@ -142,13 +142,33 @@
     across = {"row": 1 - x}
     right = {"col": lax.rem(z + 1, n_z)}
     left = {"col": lax.rem(z + n_z - 1, n_z)}
+    corners = [{"row": 1 - x, **right}, {"row": 1 - x, **left}]
     peers = [{"vec": lax.rem(y + d, n_y)} for d in range(1, n_y)]
     far = [{"row": 1 - x, "vec": lax.rem(y + d, n_y)} for d in range(n_y)]
 
+    own = pl.ds(0, ROWS)
+    other = pl.ds(ROWS, ROWS)
+    theirs = pl.ds(2 * (1 - x), 2)
+    mine = pl.ds(2 * x, 2)
+
+    def local(source, target, index):
+        copy = pltpu.make_async_copy(source, target, ls.at[index])
+        copy.start()
+        return copy
+
+    l_res = local(res, wres.at[:, own], X_RES)
+    l_ck = local(ck.at[:, :, mine], wck.at[:, :, :, own], X_CK)
+    l_adj = local(adj.at[:, mine], wadj.at[:, :, own], X_ADJ)
+    l_bits = local(bits.at[mine], wbits.at[:, own], X_BITS)
+    l_pot = local(pot, wpot.at[own], X_POT)
+    h_ck = local(ck, hck, H_CK)
+    h_adj = local(adj, hadj, H_ADJ)
+    h_bits = local(bits, hbits, H_BITS)
+
     barrier = pltpu.get_barrier_semaphore()
-    for device in [right, left] + peers + far:
+    for device in [right, left] + corners + peers + far:
         pl.semaphore_signal(barrier, inc=1, device_id=device, device_id_type=MESH)
-    pl.semaphore_wait(barrier, 2 + len(peers) + len(far))
+    pl.semaphore_wait(barrier, 4 + len(peers) + len(far))
 
     def remote(source, target, send, recv, device):
         copy = pltpu.make_async_remote_copy(
@@ -161,37 +181,22 @@
     def to_x(source, target, index):
         return remote(source, target, xs.at[index], xr.at[index], across)
 
-    theirs = pl.ds(2 * (1 - x), 2)
-    mine = pl.ds(2 * x, 2)
-    other = pl.ds(ROWS, ROWS)
-    own = pl.ds(0, ROWS)
     share = pl.ds(QUARTER * y, QUARTER)
     c_res = to_x(res.at[share], wres.at[share, other], X_RES)
     c_ck = to_x(ck.at[:, :, theirs], wck.at[:, :, :, other], X_CK)
-    c_adj = to_x(adj.at[:, theirs], wadj.at[:, :, other], X_ADJ)
-    c_bits = to_x(bits.at[theirs], wbits.at[:, other], X_BITS)
-    c_pot = to_x(pot, wpot.at[other], X_POT)
-
-    def local(source, target, index):
-        copy = pltpu.make_async_copy(source, target, ls.at[index])
-        copy.start()
-        return copy
-
-    l_res = local(res, wres.at[:, own], X_RES)
-    l_ck = local(ck.at[:, :, mine], wck.at[:, :, :, own], X_CK)
-    l_adj = local(adj.at[:, mine], wadj.at[:, :, own], X_ADJ)
-    l_bits = local(bits.at[mine], wbits.at[:, own], X_BITS)
-    l_pot = local(pot, wpot.at[own], X_POT)
 
     lane = lax.broadcasted_iota(jnp.int32, (8, LANES), 1)
 
     def rows(j):
         return pl.ds(j, 8, stride=8)
 
-    def pack(slot, j, planes):
+    def pack(slot, side, planes):
         width = LANES // len(planes)
-        zsend[0, slot, j] = pick(lane, [turn(p, width * (q + 1)) for q, p in enumerate(planes)])
-        zsend[1, slot, j] = pick(lane, [turn(p, width * q) for q, p in enumerate(planes)])
+        for i in range(ROWS // 8):
+            span = pl.ds(8 * i, 8)
+            parts = [plane(span) for plane in planes]
+            zsend[side, 0, slot, span] = pick(lane, [turn(w, width * (q + 1)) for q, w in enumerate(parts)])
+            zsend[side, 1, slot, span] = pick(lane, [turn(w, width * q) for q, w in enumerate(parts)])
 
     def unpack(pair, q, count):
         width = LANES // count
@@ -199,11 +204,13 @@
         from_right = turn(pair[1], LANES - width * q)
         return jnp.where(lane < LANES // 2, from_right, from_left)
 
-    def to_z(part, source, target):
-        return [
-            remote(source.at[d], target.at[d], zs.at[d, part], zr.at[d, part], device)
-            for d, device in enumerate((right, left))
-        ]
+    def to_z(part, slots, target, both=True):
+        copies = []
+        for side, devices, place in ((0, (right, left), own), (1, corners, other)):
+            for d, device in enumerate(devices):
+                sems = (zs.at[side, d, part], zr.at[side, d, part])
+                copies.append(remote(zsend.at[side if both else 0, d, slots], target(d, place), *sems, device))
+        return copies
 
     def fan(part, source, target, devices):
         return [
@@ -217,46 +224,65 @@
         for copy in copies:
             copy.wait()
 
+    pot_factor = scal[0]
+    twice = scal[1]
+    inv_count = scal[2]
+
     l_res.wait()
+    pack(3, 0, [lambda span, q=q: wres[QUARTER * y + q, span] for q in range(QUARTER)])
+    z_res = to_z(Z_RES, 3, lambda d, place: zres.at[d, y, place], False)
+    h_ck.wait()
+    for side, first in ((0, 2 * x), (1, 2 * (1 - x))):
+        order = [(s, k, v) for s in range(2) for k in range(2) for v in range(2)]
+        pack(0, side, [lambda span, s=s, k=k, v=v: hck[s, k, first + v, span] for s, k, v in order])
+    z_ck = to_z(Z_CK, pl.ds(0, 1), lambda d, place: zrecv.at[d, pl.ds(0, 1), place])
+
+    c_adj = to_x(adj.at[:, theirs], wadj.at[:, :, other], X_ADJ)
+    c_bits = to_x(bits.at[theirs], wbits.at[:, other], X_BITS)
+    c_pot = to_x(pot, wpot.at[other], X_POT)
+    settle([h_adj, h_bits, l_pot])
+
+    def sign_of(bit):
+        return (2 * bit - 1).astype(jnp.float32) * inv_count
+
+    def site_of(level):
+        return level.astype(jnp.float32) * pot_factor * twice
+
+    for side, first in ((0, 2 * x), (1, 2 * (1 - x))):
+        order = [(k, v) for k in range(2) for v in range(2)]
+        pack(1, side, [lambda span, k=k, v=v: hadj[k, first + v, span] for k, v in order])
+        marks = [lambda span, v=v: sign_of(hbits[first + v, span]) for v in range(2)]
+        pack(2, side, marks + [lambda span: site_of(wpot[span])] * 2)
+    z_adj = to_z(Z_ADJ, pl.ds(1, 2), lambda d, place: zrecv.at[d, pl.ds(1, 2), place])
+
     c_res.wait()
     g_rows = to_peers(V_ROWS, wres.at[share, other])
-    for j in range(DEPTH):
-        pack(3, j, [wres[QUARTER * y + q, rows(j)] for q in range(QUARTER)])
-    z_res = to_z(Z_RES, zsend.at[:, 3], zres.at[:, y])
+    settle(z_res)
+    g_halo = to_peers(V_HALO, zres.at[:, y])
 
     l_ck.wait()
     c_ck.wait()
     for j in range(DEPTH):
         planes = [wck[s, k, v, rows(j)] for s in range(2) for k in range(2) for v in range(2)]
-        pack(0, j, planes)
         for q, plane in enumerate(planes):
             s, k, v = q // 4, q // 2 % 2, q % 2
             states[s * SEG + k, v, j] = plane
             (even, odd)[k][s, v, j, 0] = plane
-    z_ck = to_z(Z_CK, zsend.at[:, pl.ds(0, 1)], zrecv.at[:, pl.ds(0, 1)])
-
-    pot_factor = scal[0]
-    twice = scal[1]
-    inv_count = scal[2]
-    settle([l_adj, l_bits, l_pot])
-    c_adj.wait()
-    c_bits.wait()
-    c_pot.wait()
+    settle(z_ck)
+    for j in range(DEPTH):
+        pair = [zrecv[d, 0, rows(j)] for d in range(2)]
+        for q in range(8):
+            s, k, v = q // 4, q // 2 % 2, q % 2
+            (even, odd)[k][s, v, j, 1] = unpack(pair, q, 8)
+
+    settle([l_adj, l_bits, c_adj, c_bits, c_pot])
     for j in range(DEPTH):
         planes = [wadj[k, v, rows(j)] for k in range(2) for v in range(2)]
-        pack(1, j, planes)
         for q, plane in enumerate(planes):
             (adj_even, adj_odd)[q // 2][q % 2, j, 0] = plane
-        sign = [(2 * wbits[v, rows(j)] - 1).astype(jnp.float32) * inv_count for v in range(2)]
-        site = wpot[rows(j)].astype(jnp.float32) * pot_factor * twice
-        pack(2, j, [sign[0], sign[1], site, site])
-        signs[0, j, 0] = sign[0]
-        signs[1, j, 0] = sign[1]
-        onsite[j, 0] = site
-    z_adj = to_z(Z_ADJ, zsend.at[:, pl.ds(1, 2)], zrecv.at[:, pl.ds(1, 2)])
-
-    settle(z_res)
-    g_halo = to_peers(V_HALO, zres.at[:, y])
+        signs[0, j, 0] = sign_of(wbits[0, rows(j)])
+        signs[1, j, 0] = sign_of(wbits[1, rows(j)])
+        onsite[j, 0] = site_of(wpot[rows(j)])
 
     def halves(value):
         high = value.astype(jnp.bfloat16)
@@ -293,18 +319,12 @@
             rwin[j, 0, e] = wres[e, rows(j)]
     weigh(0)
 
-    settle(z_ck)
-    for j in range(DEPTH):
-        pair = [zrecv[d, 0, j] for d in range(2)]
-        for q in range(8):
-            s, k, v = q // 4, q // 2 % 2, q % 2
-            (even, odd)[k][s, v, j, 1] = unpack(pair, q, 8)
     settle(z_adj)
     for j in range(DEPTH):
-        pair = [zrecv[d, 1, j] for d in range(2)]
+        pair = [zrecv[d, 1, rows(j)] for d in range(2)]
         for q in range(4):
             (adj_even, adj_odd)[q // 2][q % 2, j, 1] = unpack(pair, q, 4)
-        pair = [zrecv[d, 2, j] for d in range(2)]
+        pair = [zrecv[d, 2, rows(j)] for d in range(2)]
         signs[0, j, 1] = unpack(pair, 0, 4)
         signs[1, j, 1] = unpack(pair, 1, 4)
         onsite[j, 1] = unpack(pair, 2, 4)
@@ -351,7 +371,7 @@
     settle(g_halo)
     for j in range(DEPTH):
         for e in range(ENERGIES):
-            pair = [zres[d, e // QUARTER, j] for d in range(2)]
+            pair = [zres[d, e // QUARTER, rows(j)] for d in range(2)]
             rwin[j, 1, e] = unpack(pair, e % QUARTER, QUARTER)
     weigh(1)
 
@@ -421,14 +441,17 @@
         in_specs=[pl.BlockSpec(memory_space=pltpu.SMEM), vmem] + [pl.BlockSpec(memory_space=pl.ANY)] * 5,
         out_specs=(pl.BlockSpec(memory_space=pl.ANY),) * 2,
         scratch_shapes=[
+            pltpu.VMEM(checkpoints.shape, f32),
+            pltpu.VMEM(adjoints_in.shape, f32),
+            pltpu.VMEM(vector_bits.shape, i32),
             pltpu.VMEM((2, 2, 2, 2 * ROWS, LANES), f32),
             pltpu.VMEM((2, 2, 2 * ROWS, LANES), f32),
             pltpu.VMEM((2, 2 * ROWS, LANES), i32),
             pltpu.VMEM((2 * ROWS, LANES), i32),
             pltpu.VMEM((ENERGIES, 2 * ROWS, LANES), f32),
-            pltpu.VMEM((2, 4, DEPTH) + tile, f32),
-            pltpu.VMEM((2, 3, DEPTH) + tile, f32),
-            pltpu.VMEM((2, n_y, DEPTH) + tile, f32),
+            pltpu.VMEM((2, 2, 4, ROWS, LANES), f32),
+            pltpu.VMEM((2, 3, 2 * ROWS, LANES), f32),
+            pltpu.VMEM((2, n_y, 2 * ROWS, LANES), f32),
             pltpu.VMEM((TERMS, 2, DEPTH) + tile, f32),
             pltpu.VMEM((2, 2, DEPTH, 2) + tile, f32),
             pltpu.VMEM((2, 2, DEPTH, 2) + tile, f32),
@@ -441,11 +464,11 @@
             pltpu.VMEM((2 * ROWS, LANES), f32),
             pltpu.VMEM((2, n_y, ROWS, LANES), f32),
             pltpu.VMEM((2, 2, 2 * ROWS, LANES), f32),
+            pltpu.SemaphoreType.DMA((9,)),
             pltpu.SemaphoreType.DMA((6,)),
             pltpu.SemaphoreType.DMA((6,)),
-            pltpu.SemaphoreType.DMA((6,)),
-            pltpu.SemaphoreType.DMA((2, 3)),
-            pltpu.SemaphoreType.DMA((2, 3)),
+            pltpu.SemaphoreType.DMA((2, 2, 3)),
+            pltpu.SemaphoreType.DMA((2, 2, 3)),
             pltpu.SemaphoreType.DMA((4, n_y)),
             pltpu.SemaphoreType.DMA((4, n_y)),
         ],

time: 38.8 us -> 38.2 us (0.985)
  Pallas kernels: 31.4 us -> 30.8 us
    pallas_call x1, Pallas kernels: 31.4 us -> 30.8 us  [windowed(): pl.pallas_call(kernel, out_shape=(jax.ShapeDtypeStruct(potential_int.shap...]
where the time goes in v5:
time: 38.2 us; the launch traced here: 37.8 us
  Pallas kernels  30.8 us (81%)
  local copies, waits for them, and re-layouts  3.53 us (9%)
  between operations  2 us (5%)
  other arithmetic  1.47 us (4%)
    pallas_call x1, Pallas kernels, windowed(): pl.pallas_call(kernel, out_shape=(jax.ShapeDtypeStruct(potential_int.shap...  30.8 us
    unnamed x4, local copies, waits for them, and re-layouts  3.53 us

profile of v5, /device:TPU:0, one launch (start us, length us, event | category | flops | bytes accessed | tf_op | source)
XLA Modules:
  0.0 37.8 jit_solution(17273837535394546396)
XLA Ops:
  2.0 0.6 %pad_maximum_fusion.scal = f32[3]{0:T(128)} fusion(f32[1]{0:T(128)} %constant.8.clone.1, f32[1]{0:T(128)S(6)} %div.15, f32[1]{0:T(128)S(6)} %copy.13), kind=kLoop, calls=%fused_computation.3 | loop fusion | flops 6 | bytes 24 | tf_op jit(solution)/shard_map/stack | solution.py:431
  2.6 0.0 copy-start
  2.6 0.6 %copy-done = f32[16]{0:T(128)S(1)} copy-done((f32[16]{0:T(128)S(1)}, f32[16]{0:T(128)}, u32[]{:S(2)}) %copy-start) | copy-done | bytes 88
  3.3 0.1 sine_multiply_fusion
  3.3 0.8 %multiply_divide_fusion.coefs = f32[32,16]{1,0:T(8,128)} fusion(f32[32]{0:T(128)S(1)} %fusion, f32[16]{0:T(128)S(1)} %get-tuple-element.2, f32[16]{0:T(128)S(1)} %get-tuple-element.3, f32[32]{0:T(128)S(1)} %fusion.1), kind=kLoop, calls=%fused_computation | loop fusion | flops 1536 | bytes 2432 | tf_op jit(solution)/shard_map/div | solution.py:40
  4.1 30.8 %shard_map.95 = (f32[32,128]{1,0:T(8,128)}, f32[2,4,32,128]{3,2,1,0:T(8,128)}) custom-call(f32[3]{0:T(128)} %pad_maximum_fusion.scal, f32[32,16]{1,0:T(8,128)} %multiply_divide_fusion.coefs, f32[2,2,4,32,128]{4,3,2,1,0:T(8,128)} %ck.1, f32[2,4,32,128]{3,2,1,0:T(8,128)} %adj.1, s32[4,32,128]{2,1,0:T(8,128)} %bits.1, s32[32,128]{1,0:T(8,128)} %pot.1, ...), custom_call_target="tpu_custom_call" | custom-call | tf_op jit(solution)/shard_map/pallas_call | solution.py:435
  34.9 1.3 %copy.15 = f32[32,128]{1,0:T(8,128)} copy(f32[32,128]{1,0:T(8,128)} %get-tuple-element.6) | data formatting | bytes 32768
  36.3 1.6 %copy.16 = f32[2,4,32,128]{3,2,1,0:T(8,128)} copy(f32[2,4,32,128]{3,2,1,0:T(8,128)} %get-tuple-element.7) | data formatting | bytes 262144
  (2 shorter events, 0.1 us)
Async XLA Ops:
  2.6 0.7 %copy-start = (f32[16]{0:T(128)S(1)}, f32[16]{0:T(128)}, u32[]{:S(2)}) copy-start(f32[16]{0:T(128)} %param.13) | copy-start | bytes 196

commit v6 on v5

--- a/solution.py
+++ b/solution.py
@@ -357,13 +357,16 @@
             k = 2 + 2 * half + step
             for s in range(2):
                 for v in range(2):
+                    values = []
                     for j in range(DEPTH):
                         here, sums = beside(now.at[s], v, j)
                         for c in range(2):
-                            value = (onsite[j, c] * here[c] - twice * sums[c]) - then[s, v, j, c]
-                            then[s, v, j, c] = value
-                            if c == 0:
-                                states[s * SEG + k, v, j] = value
+                            values.append((onsite[j, c] * here[c] - twice * sums[c]) - then[s, v, j, c])
+                    for j in range(DEPTH):
+                        for c in range(2):
+                            then[s, v, j, c] = values[2 * j + c]
+                    for j in range(DEPTH):
+                        states[s * SEG + k, v, j] = values[2 * j]
         return carry
 
     lax.fori_loop(0, SEG // 2 - 1, forward, 0)
@@ -381,12 +384,16 @@
             now, then = (adj_even, adj_odd) if step == 0 else (adj_odd, adj_even)
             t = TERMS - 1 - step - 2 * half
             for v in range(2):
+                values = []
                 for j in range(DEPTH):
                     here, sums = beside(now, v, j)
                     grads[j] = grads[j] + here[0] * states[t, v, j]
                     for c in range(2):
                         source = weights[j, c, t] * signs[v, j, c]
-                        then[v, j, c] = (source + onsite[j, c] * here[c]) - (twice * sums[c] + then[v, j, c])
+                        values.append((source + onsite[j, c] * here[c]) - (twice * sums[c] + then[v, j, c]))
+                for j in range(DEPTH):
+                    for c in range(2):
+                        then[v, j, c] = values[2 * j + c]
         return tuple(grads)
 
     zero = jnp.zeros((8, LANES), jnp.float32)
@@ -473,7 +480,7 @@
             pltpu.SemaphoreType.DMA((4, n_y)),
         ],
         compiler_params=pltpu.CompilerParams(
-            collective_id=0, has_side_effects=True, vmem_limit_bytes=56 * 1024 * 1024
+            collective_id=0, has_side_effects=True, vmem_limit_bytes=537 * 1024 * 1024 // 10
         ),
     )(scal, coefficients, checkpoints, adjoints_in, vector_bits, potential_int, residual)
     return gradient, adjoint_out

time: 38.2 us -> 36.3 us (0.950)
  other arithmetic: 1.47 us -> 0.35 us
  Pallas kernels: 30.8 us -> 30.2 us
    pallas_call x1, Pallas kernels: 30.8 us -> 30.2 us  [windowed(): pl.pallas_call(kernel, out_shape=(jax.ShapeDtypeStruct(potential_int.shap...]
    div x1, other arithmetic: 0.75 us -> 0.14 us  [window_coefs(): (jackson * factor)[:, None] * cosines / (math.pi * jnp.sin(angles))[None, :]]
    another operation x1, other arithmetic: 0.59 us -> 0.08 us  [windowed(): scal = jnp.stack([pot_factor, twice, jnp.float32(inv_count)])]
    unnamed x4 -> x8, local copies, waits for them, and re-layouts: 3.53 us -> 3.47 us
where the time goes in v6:
time: 36.3 us; the launch traced here: 36 us
  Pallas kernels  30.2 us (83%)
  local copies, waits for them, and re-layouts  3.47 us (10%)
  between operations  2.03 us (6%)
    pallas_call x1, Pallas kernels, windowed(): pl.pallas_call(kernel, out_shape=(jax.ShapeDtypeStruct(potential_int.shap...  30.2 us
    unnamed x8, local copies, waits for them, and re-layouts  3.47 us

profile of v6, /device:TPU:0, one launch (start us, length us, event | category | flops | bytes accessed | tf_op | source)
XLA Modules:
  0.0 36.0 jit_solution(8956913134427225325)
XLA Ops:
  1.9 0.0 copy-start.2
  1.9 0.0 copy-start.1
  2.0 0.1 pad_maximum_fusion.scal
  2.1 0.5 %copy-done.2 = f32[16]{0:T(128)S(1)} copy-done((f32[16]{0:T(128)S(1)}, f32[16]{0:T(128)}, u32[]{:S(2)}) %copy-start.2) | copy-done | bytes 88
  2.6 0.1 sine_multiply_fusion
  2.7 0.1 multiply_divide_fusion.coefs
  2.8 0.0 copy-done.1
  2.8 0.0 copy-start
  2.8 0.8 %copy-done = s32[4,32,128]{2,1,0:T(8,128)S(1)} copy-done((s32[4,32,128]{2,1,0:T(8,128)S(1)}, s32[4,32,128]{2,1,0:T(8,128)}, u32[]{:S(2)}) %copy-start) | copy-done | bytes 65560
  3.7 30.2 %shard_map.95 = (f32[32,128]{1,0:T(8,128)S(1)}, f32[2,4,32,128]{3,2,1,0:T(8,128)}) custom-call(f32[3]{0:T(128)S(1)} %pad_maximum_fusion.scal, f32[32,16]{1,0:T(8,128)S(1)} %multiply_divide_fusion.coefs, f32[2,2,4,32,128]{4,3,2,1,0:T(8,128)} %ck.1, f32[2,4,32,128]{3,2,1,0:T(8,128)} %adj.1, s32[4,32,128]{2,1,0:T(8,128)S(1)} %copy-done, ...), custom_call_target="tpu_custom_call" | custom-call | tf_op jit(solution)/shard_map/pallas_call | solution.py:442
  33.8 0.6 %copy.15 = f32[32,128]{1,0:T(8,128)} copy(f32[32,128]{1,0:T(8,128)S(1)} %get-tuple-element.6) | data formatting | bytes 32768
  34.5 1.6 %copy.16 = f32[2,4,32,128]{3,2,1,0:T(8,128)} copy(f32[2,4,32,128]{3,2,1,0:T(8,128)} %get-tuple-element.7) | data formatting | bytes 262144
  (2 shorter events, 0.1 us)
Async XLA Ops:
  1.9 0.7 %copy-start.2 = (f32[16]{0:T(128)S(1)}, f32[16]{0:T(128)}, u32[]{:S(2)}) copy-start(f32[16]{0:T(128)} %param.13) | copy-start | bytes 196
  1.9 0.9 %copy-start.1 = (s32[32,128]{1,0:T(8,128)S(1)}, s32[32,128]{1,0:T(8,128)}, u32[]{:S(2)}) copy-start(s32[32,128]{1,0:T(8,128)} %pot.1) | copy-start | bytes 49156
  2.8 0.8 %copy-start = (s32[4,32,128]{2,1,0:T(8,128)S(1)}, s32[4,32,128]{2,1,0:T(8,128)}, u32[]{:S(2)}) copy-start(s32[4,32,128]{2,1,0:T(8,128)} %bits.1) | copy-start | bytes 196612

commit v7 on v6

--- a/solution.py
+++ b/solution.py
@@ -378,11 +378,11 @@
             rwin[j, 1, e] = unpack(pair, e % QUARTER, QUARTER)
     weigh(1)
 
-    def adjoint(half, sums_in):
+    def adjoint(part, sums_in):
         grads = list(sums_in)
-        for step in range(2):
-            now, then = (adj_even, adj_odd) if step == 0 else (adj_odd, adj_even)
-            t = TERMS - 1 - step - 2 * half
+        for step in range(4):
+            now, then = (adj_even, adj_odd) if step % 2 == 0 else (adj_odd, adj_even)
+            t = TERMS - 1 - step - 4 * part
             for v in range(2):
                 values = []
                 for j in range(DEPTH):
@@ -397,7 +397,7 @@
         return tuple(grads)
 
     zero = jnp.zeros((8, LANES), jnp.float32)
-    grads = lax.fori_loop(0, TERMS // 2, adjoint, (zero,) * DEPTH)
+    grads = lax.fori_loop(0, TERMS // 4, adjoint, (zero,) * DEPTH)
 
     for j in range(DEPTH):
         gbuf[rows(j)] = grads[j]

time: 36.3 us -> 35.7 us (0.983)
  Pallas kernels: 30.2 us -> 29.6 us
    pallas_call x1, Pallas kernels: 30.2 us -> 29.6 us  [windowed(): pl.pallas_call(kernel, out_shape=(jax.ShapeDtypeStruct(potential_int.shap...]
where the time goes in v7:
time: 35.7 us; the launch traced here: 35.5 us
  Pallas kernels  29.6 us (83%)
  local copies, waits for them, and re-layouts  3.47 us (10%)
  between operations  2.03 us (6%)
    pallas_call x1, Pallas kernels, windowed(): pl.pallas_call(kernel, out_shape=(jax.ShapeDtypeStruct(potential_int.shap...  29.6 us
    unnamed x8, local copies, waits for them, and re-layouts  3.47 us

profile of v7, /device:TPU:0, one launch (start us, length us, event | category | flops | bytes accessed | tf_op | source)
XLA Modules:
  0.0 35.5 jit_solution(6097296121611228031)
XLA Ops:
  1.9 0.0 copy-start.2
  1.9 0.0 copy-start.1
  2.0 0.1 pad_maximum_fusion.scal
  2.1 0.5 %copy-done.2 = f32[16]{0:T(128)S(1)} copy-done((f32[16]{0:T(128)S(1)}, f32[16]{0:T(128)}, u32[]{:S(2)}) %copy-start.2) | copy-done | bytes 88
  2.6 0.1 sine_multiply_fusion
  2.7 0.1 multiply_divide_fusion.coefs
  2.8 0.0 copy-done.1
  2.8 0.0 copy-start
  2.8 0.8 %copy-done = s32[4,32,128]{2,1,0:T(8,128)S(1)} copy-done((s32[4,32,128]{2,1,0:T(8,128)S(1)}, s32[4,32,128]{2,1,0:T(8,128)}, u32[]{:S(2)}) %copy-start) | copy-done | bytes 65560
  3.7 29.6 %shard_map.95 = (f32[32,128]{1,0:T(8,128)S(1)}, f32[2,4,32,128]{3,2,1,0:T(8,128)}) custom-call(f32[3]{0:T(128)S(1)} %pad_maximum_fusion.scal, f32[32,16]{1,0:T(8,128)S(1)} %multiply_divide_fusion.coefs, f32[2,2,4,32,128]{4,3,2,1,0:T(8,128)} %ck.1, f32[2,4,32,128]{3,2,1,0:T(8,128)} %adj.1, s32[4,32,128]{2,1,0:T(8,128)S(1)} %copy-done, ...), custom_call_target="tpu_custom_call" | custom-call | tf_op jit(solution)/shard_map/pallas_call | solution.py:442
  33.3 0.6 %copy.15 = f32[32,128]{1,0:T(8,128)} copy(f32[32,128]{1,0:T(8,128)S(1)} %get-tuple-element.6) | data formatting | bytes 32768
  33.9 1.6 %copy.16 = f32[2,4,32,128]{3,2,1,0:T(8,128)} copy(f32[2,4,32,128]{3,2,1,0:T(8,128)} %get-tuple-element.7) | data formatting | bytes 262144
  (2 shorter events, 0.1 us)
Async XLA Ops:
  1.9 0.7 %copy-start.2 = (f32[16]{0:T(128)S(1)}, f32[16]{0:T(128)}, u32[]{:S(2)}) copy-start(f32[16]{0:T(128)} %param.13) | copy-start | bytes 196
  1.9 0.9 %copy-start.1 = (s32[32,128]{1,0:T(8,128)S(1)}, s32[32,128]{1,0:T(8,128)}, u32[]{:S(2)}) copy-start(s32[32,128]{1,0:T(8,128)} %pot.1) | copy-start | bytes 49156
  2.8 0.8 %copy-start = (s32[4,32,128]{2,1,0:T(8,128)S(1)}, s32[4,32,128]{2,1,0:T(8,128)}, u32[]{:S(2)}) copy-start(s32[4,32,128]{2,1,0:T(8,128)} %bits.1) | copy-start | bytes 196612
